TPU v7x, 256 devices: a whole 4x4x8 slice. The times are simulated.
256 devices in a mesh: gx: 16 (over z, core), gy: 16 (over y, x).
Axes of the slice: x: 4, y: 4, z: 8, core: 2. Of those that a mesh axis runs over, the one named last changes fastest.
Arguments:
- queries: bfloat16 [16, 8192, 768], P('gy', 'gx'), may hold values from -6 to 6
- key_values: bfloat16 [2, 16, 8192, 768], P(None, 'gy', 'gx'), may hold values from -6 to 6
Outputs:
- attended: bfloat16 [16, 8192, 768], P('gy', 'gx')
All inputs are finite; a program needn't handle non-finite values.
Results may differ from a plain program's by a relative error of at most 0.0028.
The roundings to bfloat16 on the way count: a program that leaves them out, or rounds other values in their place, can miss the bound.
Values may be sent and summed in bfloat16 or wider, within the bound.
No kernel may reach another device: no remote copies, remote signals or barrier semaphores. Data moves between devices by JAX's collectives and lax.ppermute only.
A program may use at most 128 MiB of HBM per device.

v0:
```python
import functools

import jax
import jax.numpy as jnp
from jax import lax
from jax.experimental import pallas as pl
from jax.experimental.pallas import tpu as pltpu
from jax.sharding import PartitionSpec as P

HEADS = 12
HEAD = 64
WIDTH = 768
ROWS = 512
LOG2E = 1.4426950408889634
SCALE = LOG2E / 8.0
LOW = -3.0e38
BF = jnp.bfloat16
F32 = jnp.float32


def dot(a, b):
    return lax.dot_general(a, b, (((1,), (0,)), ((), ())), preferred_element_type=F32)


def dot_t(a, b):
    return lax.dot_general(a, b, (((1,), (1,)), ((), ())), preferred_element_type=F32)


def softmax_parts(scores):
    top = jnp.max(scores, axis=-1, keepdims=True)
    expo = jnp.exp2((scores - top) * SCALE)
    total = jnp.sum(expo, axis=-1, keepdims=True)
    return expo.astype(BF), 1.0 / total, top * SCALE + jnp.log(total) * LOG2E


def lanes(shape):
    return lax.broadcasted_iota(jnp.int32, shape, len(shape) - 1)


def sorted_position(index):
    return (
        (index >> 7)
        + 4 * ((index >> 5) & 3)
        + 16 * ((index >> 3) & 3)
        + 64 * ((index >> 1) & 3)
        + 256 * (index & 1)
    )


def small_pick_kernel(t_ref, q_ref, kv_ref, own_ref, one_ref, two_ref, three_ref, chunks):
    row = lax.broadcasted_iota(jnp.int32, (64, ROWS), 0)
    col = lax.broadcasted_iota(jnp.int32, (64, ROWS), 1)
    j = row & 31
    base = (row >> 5) + 16 * (j >> 3) + 64 * ((j >> 1) & 3) + 256 * (j & 1)
    zeros = jnp.zeros((32, HEAD), F32)
    for pair in range(HEADS // 2):
        onehot = (col == base + 2 * pair).astype(F32).astype(BF)
        cols = pl.ds(pair * 128, 128)
        q = dot(onehot, q_ref[0, :, cols])
        k = dot(onehot, kv_ref[0, 0, :, cols])
        v = dot(onehot, kv_ref[1, 0, :, cols])
        for side in range(2):
            head = 2 * pair + side
            rs = slice(side * 32, side * 32 + 32)
            cs = slice(side * HEAD, side * HEAD + HEAD)
            t, i = head // 3, head % 3
            chunks[t, i, 0] = jnp.concatenate([k[rs, cs], v[rs, cs]], axis=1).astype(BF)
            chunks[t, i, 1] = jnp.concatenate([q[rs, cs], zeros], axis=1).astype(BF)
    t = t_ref[0]
    own_ref[...] = chunks[t]
    one_ref[...] = chunks[t ^ 1]
    two_ref[...] = chunks[t ^ 2]
    three_ref[...] = chunks[t ^ 3]


def sort_kernel(q_ref, kv_ref, qs_ref, ks_ref, vs_ref, send_ref):
    row = lax.broadcasted_iota(jnp.int32, (ROWS, ROWS), 0)
    col = lax.broadcasted_iota(jnp.int32, (ROWS, ROWS), 1)
    onehot = (col == sorted_position(row)).astype(F32).astype(BF)
    half = lanes((128, 128)) < HEAD
    for pair in range(HEADS // 2):
        cols = pl.ds(pair * 128, 128)
        qs_ref[:, cols] = dot(onehot, q_ref[0, :, cols]).astype(BF)
        a, b = (2 * pair) % 4 * 128, (2 * pair + 1) % 4 * 128
        for n, ref in ((0, ks_ref), (1, vs_ref)):
            x = dot(onehot, kv_ref[n, 0, :, cols])
            ref[:, cols] = x.astype(BF)
            send_ref[n, :, cols] = jnp.where(half, x[a : a + 128], x[b : b + 128]).astype(BF)


def level1_kernel(q_ref, k_ref, v_ref, o_ref, e_ref):
    k, v = k_ref[...], v_ref[...]
    for c in range(2):
        rows = slice(c * 256, c * 256 + 256)
        q = q_ref[rows, :]
        half = lanes((256, 128)) < HEAD
        zero = jnp.zeros((), BF)
        outs, logs = [], []
        for side in range(2):
            mine = half if side == 0 else jnp.logical_not(half)
            p, inv, log = softmax_parts(dot_t(jnp.where(mine, q, zero), k))
            outs.append(dot(p, v) * inv)
            logs.append(log)
        o_ref[rows, :] = jnp.where(half, outs[0], outs[1])
        e_ref[rows, :] = jnp.where(half, logs[0], logs[1])


def level2_kernel(q_ref, own_ref, r1_ref, r2_ref, r3_ref, o1_ref, e1_ref, a_ref, o_ref, e_ref):
    side_id = pl.program_id(0) % 2
    zero = jnp.zeros((), BF)
    half = lanes((128, 128)) < HEAD
    half32 = lanes((32, 128)) < HEAD
    refs = (own_ref, r1_ref, r2_ref, r3_ref)
    ks = [r[0] for r in refs]
    vs = [r[1] for r in refs]
    a_ref[...] = o1_ref[...].astype(BF)
    picks = []
    for side in range(2):
        mine = half if side == 0 else jnp.logical_not(half)
        start = pl.multiple_of((side_id * 2 + side) * 128, 128)
        rows = pl.ds(start, 128)
        q = jnp.where(mine, q_ref[rows, :], zero)
        p, inv, log2 = softmax_parts(jnp.concatenate([dot_t(q, k) for k in ks], axis=1))
        out2 = sum(dot(p[:, n * 128 : n * 128 + 128], vs[n]) for n in range(4)) * inv
        e1, o1 = e1_ref[rows, :], o1_ref[rows, :]
        top = jnp.maximum(e1, log2)
        w1, w2 = jnp.exp2(e1 - top), jnp.exp2(log2 - top)
        den = w1 + w2
        o = (w1 * o1 + w2 * out2) / den
        e = top + jnp.log(den) * LOG2E
        a_ref[rows, :] = jnp.where(mine, o.astype(BF), a_ref[rows, :])
        picks.append((o, e))
    low = pl.program_id(0) // 2
    for n in range(3):

        @pl.when(low == n)
        def _():
            rs = slice(n * 32, n * 32 + 32)
            o_ref[...] = jnp.where(half32, picks[0][0][rs], picks[1][0][rs])
            e_ref[...] = jnp.where(half32, picks[0][1][rs], picks[1][1][rs])


def regroup_kernel(own_ref, r1_ref, r2_ref, r3_ref, kv_ref, q_ref, kv4_ref, q4_ref):
    refs = (own_ref, r1_ref, r2_ref, r3_ref)
    for i in range(3):
        kv = [r[i, 0] for r in refs]
        q = [r[i, 1] for r in refs]
        for n in range(4):
            kv_ref[i, n * 32 : n * 32 + 32, :] = kv[n]
            q_ref[i, n * 32 : n * 32 + 32, :] = q[n]
        kv4_ref[i] = jnp.concatenate([x.astype(F32)[:8] for x in kv], axis=0).astype(BF)
        q4_ref[i] = jnp.concatenate([x.astype(F32)[:8] for x in q], axis=0).astype(BF)


def level3_kernel(q_ref, kv0_ref, kv1_ref, kv2_ref, kv3_ref, o_ref):
    half = lanes((128, 128)) < HEAD
    for i in range(3):
        kvs = [r[i] for r in (kv0_ref, kv1_ref, kv2_ref, kv3_ref)]
        p, inv, log = softmax_parts(jnp.concatenate([dot_t(q_ref[i], x) for x in kvs], axis=1))
        out = sum(dot(p[:, n * 128 : n * 128 + 128], kvs[n]) for n in range(4)) * inv
        o_ref[i] = jnp.where(half, log, out)


def mix(o1, e1, o2, e2):
    top = jnp.maximum(e1, e2)
    w1, w2 = jnp.exp2(e1 - top), jnp.exp2(e2 - top)
    den = w1 + w2
    return (w1 * o1 + w2 * o2) / den, top + jnp.log(den) * LOG2E


def level45_kernel(
    t_ref, q0_ref, q1_ref, q2_ref, q3_ref, kv0_ref, kv1_ref, kv2_ref, kv3_ref, l3_ref,
    own_ref, one_ref, two_ref, three_ref, fifth_ref,
):
    t, y = t_ref[0], t_ref[1]
    half = lanes((128, 128)) < HEAD
    half32 = lanes((32, 128)) < HEAD
    in_five = (lanes((128, 512)) & 7) < 2
    outs = (own_ref, one_ref, two_ref, three_ref)
    fifth_ref[...] = jnp.zeros_like(fifth_ref)
    for i in range(3):
        kvs = [r[i] for r in (kv0_ref, kv1_ref, kv2_ref, kv3_ref)]
        q = jnp.concatenate([r[i] for r in (q0_ref, q1_ref, q2_ref, q3_ref)], axis=0)
        scores = jnp.concatenate([dot_t(q, x) for x in kvs], axis=1)
        p, inv, log4 = softmax_parts(scores[:32])
        out4 = sum(dot(p[:, n * 128 : n * 128 + 128], kvs[n]) for n in range(4)) * inv
        l3 = l3_ref[i]
        for n in range(4):
            old = l3[n * 32 : n * 32 + 32]
            rs = slice(n * 8, n * 8 + 8)
            head8 = old[:8]
            log3 = head8[:, :1]
            o, e = mix(head8, log3, out4[rs], log4[rs])
            outs[n][i, :8, :] = jnp.where(half[:8], e, o)
            outs[n][i, 8:, :] = old[8:]
        p, inv, log5 = softmax_parts(jnp.where(in_five, scores, LOW))
        out5 = sum(dot(p[:, n * 128 : n * 128 + 128], kvs[n]) for n in range(4)) * inv
        both = jnp.where(half, log5, out5)
        for m in range(4):
            for n in range(4):
                slot = (t ^ n) * 4 + (y ^ m)
                fifth_ref[slot, 2 * i : 2 * i + 2, :] = both[m * 32 + n * 8 : m * 32 + n * 8 + 2]


def final_kernel(
    t_ref, a_ref, o_ref, e_ref, own_ref, one_ref, two_ref, three_ref, fifth_ref, out_ref, rows_ref, back
):
    t = t_ref[0]
    for n, r in enumerate((own_ref, one_ref, two_ref, three_ref)):
        back[n] = r[...]
    half = lanes((32, 128)) < HEAD
    half128 = lanes((128, 128)) < HEAD
    rows_ref[...] = a_ref[...]
    for head in range(HEADS):
        source, i = head // 3, head % 3
        got = back[t ^ source, i]
        pieces = [fifth_ref[source * 4 + m, 2 * i : 2 * i + 2, :] for m in range(4)]
        e, o = got[:, :HEAD], got[:, HEAD:]
        e2, o2 = e[:2], o[:2]
        logs = [x[:, :HEAD] for x in pieces]
        top = functools.reduce(jnp.maximum, logs, e2)
        w = [jnp.exp2(x - top) for x in logs]
        w2 = jnp.exp2(e2 - top)
        den = sum(w, w2)
        num = sum((wi * x[:, HEAD:] for wi, x in zip(w, pieces)), w2 * o2)
        o = jnp.concatenate([num / den, o[2:]], axis=0)
        e = jnp.concatenate([top + jnp.log(den) * LOG2E, e[2:]], axis=0)
        cols = slice(head * HEAD, head * HEAD + HEAD)
        mixed, _ = mix(o_ref[:, cols], e_ref[:, cols], o, e)
        base = head % 4 * 128 + head // 4 * 32
        rows_ref[base : base + 32, cols] = mixed.astype(BF)
    row = lax.broadcasted_iota(jnp.int32, (ROWS, ROWS), 0)
    col = lax.broadcasted_iota(jnp.int32, (ROWS, ROWS), 1)
    onehot = (row == sorted_position(col)).astype(F32).astype(BF)
    for pair in range(HEADS // 2):
        cols = pl.ds(pair * 128, 128)
        out_ref[0, :, cols] = dot(onehot, rows_ref[:, cols]).astype(BF)


VMEM = pl.BlockSpec(memory_space=pltpu.VMEM)
SMEM = pl.BlockSpec(memory_space=pltpu.SMEM)


def call(kernel, outs, in_specs=None, scratch=(), flops=0, nbytes=0, limit=24, **more):
    def run(*args):
        specs = in_specs if in_specs is not None else [VMEM] * len(args)
        out_specs = more.pop("out_specs", None) or [VMEM] * len(outs)
        return pl.pallas_call(
            kernel,
            out_shape=[jax.ShapeDtypeStruct(s, d) for s, d in outs],
            in_specs=specs,
            out_specs=out_specs,
            scratch_shapes=list(scratch),
            cost_estimate=pl.CostEstimate(flops=flops, bytes_accessed=nbytes, transcendentals=0),
            compiler_params=pltpu.CompilerParams(vmem_limit_bytes=limit << 20),
            **more,
        )(*args)

    return run


def permute(x, axis, partner):
    return lax.ppermute(x, axis, [(i, partner(i)) for i in range(lax.axis_size(axis))])


def per_device(queries, key_values):
    gx, gy = lax.axis_index("gx"), lax.axis_index("gy")
    place = jnp.stack([gx & 3, gy >> 2]).astype(jnp.int32)

    chunk = ((3, 2, 32, 128), BF)
    own, c1, c2, c3 = call(
        small_pick_kernel, [chunk] * 4, [SMEM, VMEM, VMEM], [pltpu.VMEM((4, 3, 2, 32, 128), BF)],
        nbytes=3 << 20,
    )(place, queries, key_values)
    g = [own] + [permute(c, "gx", lambda i, n=n: i ^ n) for n, c in ((1, c1), (2, c2), (3, c3))]

    qs, ks, vs, send2 = call(
        sort_kernel, [((ROWS, WIDTH), BF)] * 3 + [((2, 128, WIDTH), BF)], nbytes=6 << 20
    )(queries, key_values)

    block = pl.BlockSpec((ROWS, 128), lambda i: (0, i))
    o1, e1 = call(
        level1_kernel, [((ROWS, WIDTH), F32)] * 2, [block] * 3, out_specs=[block] * 2, grid=(6,),
        flops=4 * 512 * 512 * 64 * 12 * 8, nbytes=6 << 20,
    )(qs, ks, vs)

    kv3, q3, kv4, q4 = call(
        regroup_kernel,
        [((3, 128, 128), BF), ((3, 128, 128), BF), ((3, 32, 128), BF), ((3, 32, 128), BF)],
        nbytes=1 << 19,
    )(*g)
    z4 = [kv4] + [permute(kv4, "gx", lambda i, n=n: i ^ n) for n in (8, 4, 12)]
    q5 = [q4] + [permute(q4, "gy", lambda i, n=n: i ^ 4 * n) for n in (1, 2, 3)]
    kv4_all = jnp.concatenate(z4, axis=1)
    x4 = [kv4_all] + [permute(kv4_all, "gy", lambda i, n=n: i ^ n) for n in (1, 2, 3)]
    z3 = [kv3] + [permute(kv3, "gx", lambda i, n=n: i ^ n) for n in (8, 4, 12)]

    far2 = permute(send2, "gx", lambda i: i ^ 2)
    near2 = permute(send2, "gx", lambda i: i ^ 1)
    other2 = permute(far2, "gx", lambda i: i ^ 1)
    pairs = pl.BlockSpec((2, 128, 128), lambda i: (0, 0, i))
    narrow = pl.BlockSpec((32, 128), lambda i: (0, i))
    a12, o12, e12 = call(
        level2_kernel, [((ROWS, WIDTH), BF), ((32, WIDTH), F32), ((32, WIDTH), F32)],
        [block] + [pairs] * 4 + [block] * 2, out_specs=[block, narrow, narrow], grid=(6,),
        flops=4 * 128 * 512 * 64 * 12 * 8, nbytes=6 << 20,
    )(qs, send2, far2, near2, other2, o1, e1)

    (l3,) = call(level3_kernel, [((3, 128, 128), F32)], nbytes=1 << 20)(q3, *z3)
    part = ((3, 32, 128), F32)
    p0, p1, p2, p3, fifth = call(
        level45_kernel, [part] * 4 + [((16, 8, 128), F32)], [SMEM] + [VMEM] * 9, nbytes=1 << 20
    )(place, *q5, *x4, l3)
    back = [p0] + [permute(x, "gx", lambda i, n=n: i ^ n) for n, x in ((1, p1), (2, p2), (3, p3))]
    groups = [
        [(4 * zg + t) * 16 + (4 * y + x) for t in range(4) for y in range(4)]
        for zg in range(4)
        for x in range(4)
    ]
    fifth = lax.all_to_all(fifth, ("gx", "gy"), 0, 0, axis_index_groups=groups)
    (out,) = call(
        final_kernel, [((1, ROWS, WIDTH), BF)], [SMEM] + [VMEM] * 8,
        [pltpu.VMEM((ROWS, WIDTH), BF), pltpu.VMEM((4, 3, 32, 128), F32)], nbytes=4 << 20,
    )(place, a12, o12, e12, *back, fifth)
    return out


def solution(mesh):
    return jax.shard_map(
        per_device,
        mesh=mesh,
        in_specs=(P("gy", "gx", None), P(None, "gy", "gx", None)),
        out_specs=P("gy", "gx", None),
        check_vma=False,
    )
```

profile of v0, /device:TPU:1, one launch (start us, length us, event | category | flops | bytes accessed | tf_op | source)
XLA Modules:
  0.0 82.9 jit_solution(15064499489805585617)
XLA Ops:
  0.1 1.4 %copy-done = bf16[2,1,512,768]{3,2,1,0:T(8,128)(2,1)S(1)} copy-done((bf16[2,1,512,768]{3,2,1,0:T(8,128)(2,1)S(1)}, bf16[2,1,512,768]{3,2,1,0:T(8,128)(2,1)}, u32[]{:S(2)}) %copy-start) | copy-done | bytes 1572888
  3.7 3.3 %collective-permute-start.3 = (bf16[3,2,32,128]{3,2,1,0:T(8,128)(2,1)S(1)}, bf16[3,2,32,128]{3,2,1,0:T(8,128)(2,1)S(1)}, u32[]{:S(2)}, u32[]{:S(2)}) collective-permute-start(bf16[3,2,32,128]{3,2,1,0:T(8,128)(2,1)S(1)} %get-tuple-element.37), channel_id=1, source_target_pairs={{0,16},{16,0},{32,48},{48,32},{64,80},{80,64},{96,112},{112,96},{1... | collective-permute-start | bytes 147464 | tf_op jit(solution)/shard_map/ppermute | solution.py:263
  7.1 1.7 %collective-permute-start.5 = (bf16[3,2,32,128]{3,2,1,0:T(8,128)(2,1)S(1)}, bf16[3,2,32,128]{3,2,1,0:T(8,128)(2,1)S(1)}, u32[]{:S(2)}, u32[]{:S(2)}) collective-permute-start(bf16[3,2,32,128]{3,2,1,0:T(8,128)(2,1)S(1)} %get-tuple-element.39), channel_id=1, source_target_pairs={{0,48},{16,32},{32,16},{48,0},{64,112},{80,96},{96,80},{112,64},{1... | collective-permute-start | bytes 147464 | tf_op jit(solution)/shard_map/ppermute | solution.py:263
  8.8 2.7 %shard_map.28 = (bf16[512,768]{1,0:T(8,128)(2,1)S(1)}, bf16[512,768]{1,0:T(8,128)(2,1)S(1)}, bf16[512,768]{1,0:T(8,128)(2,1)S(1)}, bf16[2,128,768]{2,1,0:T(8,128)(2,1)S(1)}) custom-call(bf16[1,512,768]{2,1,0:T(8,128)(2,1)S(1)} %copy-done.1, bf16[2,1,512,768]{3,2,1,0:T(8,128)(2,1)S(1)} %copy-done), custom_call_target="tpu_custom_call" | custom-call | bytes 6291456 | tf_op jit(solution)/shard_map/pallas_call | solution.py:248
  11.6 6.0 %collective-permute-start.9 = (bf16[3,32,128]{2,1,0:T(8,128)(2,1)S(1)}, bf16[3,32,128]{2,1,0:T(8,128)(2,1)S(1)}, u32[]{:S(2)}, u32[]{:S(2)}) collective-permute-start(bf16[3,32,128]{2,1,0:T(8,128)(2,1)S(1)} %get-tuple-element.41), channel_id=1, source_target_pairs={{0,128},{16,144},{32,160},{48,176},{64,192},{80,208},{96,224},{112... | collective-permute-start | bytes 73736 | tf_op jit(solution)/shard_map/ppermute | solution.py:263
  17.6 1.2 %collective-permute-start.10 = (bf16[3,32,128]{2,1,0:T(8,128)(2,1)S(1)}, bf16[3,32,128]{2,1,0:T(8,128)(2,1)S(1)}, u32[]{:S(2)}, u32[]{:S(2)}) collective-permute-start(bf16[3,32,128]{2,1,0:T(8,128)(2,1)S(1)} %get-tuple-element.41), channel_id=1, source_target_pairs={{0,64},{16,80},{32,96},{48,112},{64,0},{80,16},{96,32},{112,48},{1... | collective-permute-start | bytes 73736 | tf_op jit(solution)/shard_map/ppermute | solution.py:263
  18.8 1.3 %collective-permute-start.6 = (bf16[3,32,128]{2,1,0:T(8,128)(2,1)S(1)}, bf16[3,32,128]{2,1,0:T(8,128)(2,1)S(1)}, u32[]{:S(2)}, u32[]{:S(2)}) collective-permute-start(bf16[3,32,128]{2,1,0:T(8,128)(2,1)S(1)} %get-tuple-element.40.q0_ref), channel_id=1, source_target_pairs={{0,4},{1,5},{2,6},{3,7},{4,0},{5,1},{6,2},{7,3},{8,12},{9,13},{10,... | collective-permute-start | bytes 73736 | tf_op jit(solution)/shard_map/ppermute | solution.py:263
  20.1 7.2 %collective-permute-done.9 = bf16[3,32,128]{2,1,0:T(8,128)(2,1)S(1)} collective-permute-done((bf16[3,32,128]{2,1,0:T(8,128)(2,1)S(1)}, bf16[3,32,128]{2,1,0:T(8,128)(2,1)S(1)}, u32[]{:S(2)}, u32[]{:S(2)}) %collective-permute-start.9) | collective-permute-done | bytes 24608 | tf_op jit(solution)/shard_map/ppermute | solution.py:263
  27.3 2.9 %collective-permute-start.7 = (bf16[3,32,128]{2,1,0:T(8,128)(2,1)S(1)}, bf16[3,32,128]{2,1,0:T(8,128)(2,1)S(1)}, u32[]{:S(2)}, u32[]{:S(2)}) collective-permute-start(bf16[3,32,128]{2,1,0:T(8,128)(2,1)S(1)} %get-tuple-element.40.q0_ref), channel_id=1, source_target_pairs={{0,8},{1,9},{2,10},{3,11},{4,12},{5,13},{6,14},{7,15},{8,0},{9,1},... | collective-permute-start | bytes 73736 | tf_op jit(solution)/shard_map/ppermute | solution.py:263
  30.4 2.9 %collective-permute-start.16 = (bf16[3,128,128]{2,1,0:T(8,128)(2,1)S(1)}, bf16[3,128,128]{2,1,0:T(8,128)(2,1)S(1)}, u32[]{:S(2)}, u32[]{:S(2)}) collective-permute-start(bf16[3,128,128]{2,1,0:T(8,128)(2,1)S(1)} %get-tuple-element.43.kv0_ref), channel_id=1, source_target_pairs={{0,64},{16,80},{32,96},{48,112},{64,0},{80,16},{96,32},{112,48},{1... | collective-permute-start | bytes 294920 | tf_op jit(solution)/shard_map/ppermute | solution.py:263
  33.3 2.8 %collective-permute-start.17 = (bf16[3,128,128]{2,1,0:T(8,128)(2,1)S(1)}, bf16[3,128,128]{2,1,0:T(8,128)(2,1)S(1)}, u32[]{:S(2)}, u32[]{:S(2)}) collective-permute-start(bf16[3,128,128]{2,1,0:T(8,128)(2,1)S(1)} %get-tuple-element.43.kv0_ref), channel_id=1, source_target_pairs={{0,192},{16,208},{32,224},{48,240},{64,128},{80,144},{96,160},{112... | collective-permute-start | bytes 294920 | tf_op jit(solution)/shard_map/ppermute | solution.py:263
  36.9 3.4 %collective-permute-done.8.q3_ref = bf16[3,32,128]{2,1,0:T(8,128)(2,1)S(1)} collective-permute-done((bf16[3,32,128]{2,1,0:T(8,128)(2,1)S(1)}, bf16[3,32,128]{2,1,0:T(8,128)(2,1)S(1)}, u32[]{:S(2)}, u32[]{:S(2)}) %collective-permute-start.8) | collective-permute-done | bytes 24608 | tf_op jit(solution)/shard_map/ppermute | solution.py:263
  40.3 3.8 %collective-permute-start.1 = (bf16[2,128,768]{2,1,0:T(8,128)(2,1)S(1)}, bf16[2,128,768]{2,1,0:T(8,128)(2,1)S(1)}, u32[]{:S(2)}, u32[]{:S(2)}) collective-permute-start(bf16[2,128,768]{2,1,0:T(8,128)(2,1)S(1)} %get-tuple-element.28.own_ref), channel_id=1, source_target_pairs={{0,16},{16,0},{32,48},{48,32},{64,80},{80,64},{96,112},{112,96},{1... | collective-permute-start | bytes 1179656 | tf_op jit(solution)/shard_map/ppermute | solution.py:263
  44.1 1.2 %collective-permute-start.12 = (bf16[3,128,128]{2,1,0:T(8,128)(2,1)S(1)}, bf16[3,128,128]{2,1,0:T(8,128)(2,1)S(1)}, u32[]{:S(2)}, u32[]{:S(2)}) collective-permute-start(bf16[3,128,128]{2,1,0:T(8,128)(2,1)S(1)} %constant_dynamic-update-slice_fusion.kv0_ref), channel_id=1, source_target_pairs={{0,1},{1,0},{2,3},{3,2},{4,5},{5,4},{6,7},{7,6},{8,9},{9,8},{10,11... | collective-permute-start | bytes 294920 | tf_op jit(solution)/shard_map/ppermute | solution.py:263
  45.3 2.5 %collective-permute-start.13 = (bf16[3,128,128]{2,1,0:T(8,128)(2,1)S(1)}, bf16[3,128,128]{2,1,0:T(8,128)(2,1)S(1)}, u32[]{:S(2)}, u32[]{:S(2)}) collective-permute-start(bf16[3,128,128]{2,1,0:T(8,128)(2,1)S(1)} %constant_dynamic-update-slice_fusion.kv0_ref), channel_id=1, source_target_pairs={{0,2},{1,3},{2,0},{3,1},{4,6},{5,7},{6,4},{7,5},{8,10},{9,11},{10,... | collective-permute-start | bytes 294920 | tf_op jit(solution)/shard_map/ppermute | solution.py:263
  48.8 9.2 %shard_map.29 = (f32[512,768]{1,0:T(8,128)S(1)}, f32[512,768]{1,0:T(8,128)S(1)}) custom-call(bf16[512,768]{1,0:T(8,128)(2,1)S(1)} %get-tuple-element.27.q_ref, bf16[512,768]{1,0:T(8,128)(2,1)S(1)} %get-tuple-element.29.k_ref, bf16[512,768]{1,0:T(8,128)(2,1)S(1)} %get-tuple-element.30.v_ref), custom_call_target="tpu_custom_call" | custom-call | flops 6442450944 | bytes 6291456 | tf_op jit(solution)/shard_map/pallas_call | solution.py:248
  58.0 1.2 %copy-done.4 = f32[512,768]{1,0:T(8,128)} copy-done((f32[512,768]{1,0:T(8,128)}, f32[512,768]{1,0:T(8,128)S(1)}, u32[]{:S(2)}) %copy-start.4) | copy-done | bytes 1572888
  61.5 2.4 %shard_map.34 = (f32[3,32,128]{2,1,0:T(8,128)S(1)}, f32[3,32,128]{2,1,0:T(8,128)S(1)}, f32[3,32,128]{2,1,0:T(8,128)S(1)}, f32[3,32,128]{2,1,0:T(8,128)S(1)}, f32[16,8,128]{2,1,0:T(8,128)}) custom-call(s32[2]{0:T(128)S(1)} %pad_add_fusion.t_ref, bf16[3,32,128]{2,1,0:T(8,128)(2,1)S(1)} %get-tuple-element.40.q0_ref, ...), custom_call_target="tpu_custom_call" | custom-call | bytes 1048576 | tf_op jit(solution)/shard_map/pallas_call | solution.py:248
  64.3 1.7 %collective-permute-start.20 = (f32[3,32,128]{2,1,0:T(8,128)S(1)}, f32[3,32,128]{2,1,0:T(8,128)S(1)}, u32[]{:S(2)}, u32[]{:S(2)}) collective-permute-start(f32[3,32,128]{2,1,0:T(8,128)S(1)} %get-tuple-element.47), channel_id=1, source_target_pairs={{0,48},{16,32},{32,16},{48,0},{64,112},{80,96},{96,80},{112,64},{1... | collective-permute-start | bytes 147464 | tf_op jit(solution)/shard_map/ppermute | solution.py:263
  66.0 3.4 %all-to-all-start = ((f32[16,8,128]{2,1,0:T(8,128)}), f32[16,8,128]{2,1,0:T(8,128)S(1)}, u32[]{:S(2)}, u32[]{:S(2)}) async-start(f32[16,8,128]{2,1,0:T(8,128)} %get-tuple-element.48), calls=%async_computation | async-start | bytes 131072 | tf_op jit(solution)/shard_map/all_to_all | solution.py:320
  71.2 1.4 %copy-done.5 = f32[512,768]{1,0:T(8,128)S(1)} copy-done((f32[512,768]{1,0:T(8,128)S(1)}, f32[512,768]{1,0:T(8,128)}, u32[]{:S(2)}) %copy-start.5) | copy-done | bytes 1572888
  72.6 1.4 %copy-done.7 = f32[512,768]{1,0:T(8,128)S(1)} copy-done((f32[512,768]{1,0:T(8,128)S(1)}, f32[512,768]{1,0:T(8,128)}, u32[]{:S(2)}) %copy-start.7) | copy-done | bytes 1572888
  74.0 6.0 %shard_map.30 = (bf16[512,768]{1,0:T(8,128)(2,1)S(1)}, f32[32,768]{1,0:T(8,128)S(1)}, f32[32,768]{1,0:T(8,128)S(1)}) custom-call(bf16[512,768]{1,0:T(8,128)(2,1)S(1)} %get-tuple-element.27.q_ref, bf16[2,128,768]{2,1,0:T(8,128)(2,1)S(1)} %get-tuple-element.28.own_ref, bf16[2,128,768]{2,1,0:T(8,128)(2,1)S(1)} %collective-permute-done.r1_ref, ...), custom_call_target="tpu_custom_call" | custom-call | flops 1610612736 | bytes 6291456 | tf_op jit(solution)/shard_map/pallas_call | solution.py:248
  80.0 2.8 %shard_map.35 = bf16[1,512,768]{2,1,0:T(8,128)(2,1)} custom-call(s32[2]{0:T(128)S(1)} %pad_add_fusion.t_ref, bf16[512,768]{1,0:T(8,128)(2,1)S(1)} %get-tuple-element.33.a_ref, f32[32,768]{1,0:T(8,128)S(1)} %get-tuple-element.34.o_ref, f32[32,768]{1,0:T(8,128)S(1)} %get-tuple-element.35.e_ref, f32[3,32,128]{2,1,0:T(8,128)S(1)} %get-tuple-element.44.own_ref, ...), custom_call_target="tpu_custom_call" | custom-call | bytes 4194304 | tf_op jit(solution)/shard_map/pallas_call | solution.py:248
  (49 shorter events, 8.9 us)
Async XLA Ops:
  0.1 1.4 %copy-start = (bf16[2,1,512,768]{3,2,1,0:T(8,128)(2,1)S(1)}, bf16[2,1,512,768]{3,2,1,0:T(8,128)(2,1)}, u32[]{:S(2)}) copy-start(bf16[2,1,512,768]{3,2,1,0:T(8,128)(2,1)} %kv_ref.3) | copy-start | bytes 4718596
  3.7 7.8 %collective-permute-start.3 = (bf16[3,2,32,128]{3,2,1,0:T(8,128)(2,1)S(1)}, bf16[3,2,32,128]{3,2,1,0:T(8,128)(2,1)S(1)}, u32[]{:S(2)}, u32[]{:S(2)}) collective-permute-start(bf16[3,2,32,128]{3,2,1,0:T(8,128)(2,1)S(1)} %get-tuple-element.37), channel_id=1, source_target_pairs={{0,16},{16,0},{32,48},{48,32},{64,80},{80,64},{96,112},{112,96},{1... | collective-permute-start | bytes 147464 | tf_op jit(solution)/shard_map/ppermute | solution.py:263
  7.1 4.5 %collective-permute-start.4 = (bf16[3,2,32,128]{3,2,1,0:T(8,128)(2,1)S(1)}, bf16[3,2,32,128]{3,2,1,0:T(8,128)(2,1)S(1)}, u32[]{:S(2)}, u32[]{:S(2)}) collective-permute-start(bf16[3,2,32,128]{3,2,1,0:T(8,128)(2,1)S(1)} %get-tuple-element.38), channel_id=1, source_target_pairs={{0,32},{16,48},{32,0},{48,16},{64,96},{80,112},{96,64},{112,80},{1... | collective-permute-start | bytes 147464 | tf_op jit(solution)/shard_map/ppermute | solution.py:263
  7.1 4.5 %collective-permute-start.5 = (bf16[3,2,32,128]{3,2,1,0:T(8,128)(2,1)S(1)}, bf16[3,2,32,128]{3,2,1,0:T(8,128)(2,1)S(1)}, u32[]{:S(2)}, u32[]{:S(2)}) collective-permute-start(bf16[3,2,32,128]{3,2,1,0:T(8,128)(2,1)S(1)} %get-tuple-element.39), channel_id=1, source_target_pairs={{0,48},{16,32},{32,16},{48,0},{64,112},{80,96},{96,80},{112,64},{1... | collective-permute-start | bytes 147464 | tf_op jit(solution)/shard_map/ppermute | solution.py:263
  11.5 36.5 %collective-permute-start = (bf16[2,128,768]{2,1,0:T(8,128)(2,1)S(1)}, bf16[2,128,768]{2,1,0:T(8,128)(2,1)S(1)}, u32[]{:S(2)}, u32[]{:S(2)}) collective-permute-start(bf16[2,128,768]{2,1,0:T(8,128)(2,1)S(1)} %get-tuple-element.28.own_ref), channel_id=1, source_target_pairs={{0,32},{16,48},{32,0},{48,16},{64,96},{80,112},{96,64},{112,80},{1... | collective-permute-start | bytes 1179656 | tf_op jit(solution)/shard_map/ppermute | solution.py:263
  11.6 15.7 %collective-permute-start.9 = (bf16[3,32,128]{2,1,0:T(8,128)(2,1)S(1)}, bf16[3,32,128]{2,1,0:T(8,128)(2,1)S(1)}, u32[]{:S(2)}, u32[]{:S(2)}) collective-permute-start(bf16[3,32,128]{2,1,0:T(8,128)(2,1)S(1)} %get-tuple-element.41), channel_id=1, source_target_pairs={{0,128},{16,144},{32,160},{48,176},{64,192},{80,208},{96,224},{112... | collective-permute-start | bytes 73736 | tf_op jit(solution)/shard_map/ppermute | solution.py:263
  17.6 12.6 %collective-permute-start.10 = (bf16[3,32,128]{2,1,0:T(8,128)(2,1)S(1)}, bf16[3,32,128]{2,1,0:T(8,128)(2,1)S(1)}, u32[]{:S(2)}, u32[]{:S(2)}) collective-permute-start(bf16[3,32,128]{2,1,0:T(8,128)(2,1)S(1)} %get-tuple-element.41), channel_id=1, source_target_pairs={{0,64},{16,80},{32,96},{48,112},{64,0},{80,16},{96,32},{112,48},{1... | collective-permute-start | bytes 73736 | tf_op jit(solution)/shard_map/ppermute | solution.py:263
  18.8 11.6 %collective-permute-start.11 = (bf16[3,32,128]{2,1,0:T(8,128)(2,1)S(1)}, bf16[3,32,128]{2,1,0:T(8,128)(2,1)S(1)}, u32[]{:S(2)}, u32[]{:S(2)}) collective-permute-start(bf16[3,32,128]{2,1,0:T(8,128)(2,1)S(1)} %get-tuple-element.41), channel_id=1, source_target_pairs={{0,192},{16,208},{32,224},{48,240},{64,128},{80,144},{96,160},{112... | collective-permute-start | bytes 73736 | tf_op jit(solution)/shard_map/ppermute | solution.py:263
  18.8 14.5 %collective-permute-start.6 = (bf16[3,32,128]{2,1,0:T(8,128)(2,1)S(1)}, bf16[3,32,128]{2,1,0:T(8,128)(2,1)S(1)}, u32[]{:S(2)}, u32[]{:S(2)}) collective-permute-start(bf16[3,32,128]{2,1,0:T(8,128)(2,1)S(1)} %get-tuple-element.40.q0_ref), channel_id=1, source_target_pairs={{0,4},{1,5},{2,6},{3,7},{4,0},{5,1},{6,2},{7,3},{8,12},{9,13},{10,... | collective-permute-start | bytes 73736 | tf_op jit(solution)/shard_map/ppermute | solution.py:263
  27.3 8.8 %collective-permute-start.7 = (bf16[3,32,128]{2,1,0:T(8,128)(2,1)S(1)}, bf16[3,32,128]{2,1,0:T(8,128)(2,1)S(1)}, u32[]{:S(2)}, u32[]{:S(2)}) collective-permute-start(bf16[3,32,128]{2,1,0:T(8,128)(2,1)S(1)} %get-tuple-element.40.q0_ref), channel_id=1, source_target_pairs={{0,8},{1,9},{2,10},{3,11},{4,12},{5,13},{6,14},{7,15},{8,0},{9,1},... | collective-permute-start | bytes 73736 | tf_op jit(solution)/shard_map/ppermute | solution.py:263
  30.2 13.8 %collective-permute-start.15 = (bf16[3,128,128]{2,1,0:T(8,128)(2,1)S(1)}, bf16[3,128,128]{2,1,0:T(8,128)(2,1)S(1)}, u32[]{:S(2)}, u32[]{:S(2)}) collective-permute-start(bf16[3,128,128]{2,1,0:T(8,128)(2,1)S(1)} %get-tuple-element.43.kv0_ref), channel_id=1, source_target_pairs={{0,128},{16,144},{32,160},{48,176},{64,192},{80,208},{96,224},{112... | collective-permute-start | bytes 294920 | tf_op jit(solution)/shard_map/ppermute | solution.py:263
  30.4 14.9 %collective-permute-start.16 = (bf16[3,128,128]{2,1,0:T(8,128)(2,1)S(1)}, bf16[3,128,128]{2,1,0:T(8,128)(2,1)S(1)}, u32[]{:S(2)}, u32[]{:S(2)}) collective-permute-start(bf16[3,128,128]{2,1,0:T(8,128)(2,1)S(1)} %get-tuple-element.43.kv0_ref), channel_id=1, source_target_pairs={{0,64},{16,80},{32,96},{48,112},{64,0},{80,16},{96,32},{112,48},{1... | collective-permute-start | bytes 294920 | tf_op jit(solution)/shard_map/ppermute | solution.py:263
  33.3 14.4 %collective-permute-start.17 = (bf16[3,128,128]{2,1,0:T(8,128)(2,1)S(1)}, bf16[3,128,128]{2,1,0:T(8,128)(2,1)S(1)}, u32[]{:S(2)}, u32[]{:S(2)}) collective-permute-start(bf16[3,128,128]{2,1,0:T(8,128)(2,1)S(1)} %get-tuple-element.43.kv0_ref), channel_id=1, source_target_pairs={{0,192},{16,208},{32,224},{48,240},{64,128},{80,144},{96,160},{112... | collective-permute-start | bytes 294920 | tf_op jit(solution)/shard_map/ppermute | solution.py:263
  36.1 4.2 %collective-permute-start.8 = (bf16[3,32,128]{2,1,0:T(8,128)(2,1)S(1)}, bf16[3,32,128]{2,1,0:T(8,128)(2,1)S(1)}, u32[]{:S(2)}, u32[]{:S(2)}) collective-permute-start(bf16[3,32,128]{2,1,0:T(8,128)(2,1)S(1)} %get-tuple-element.40.q0_ref), channel_id=1, source_target_pairs={{0,12},{1,13},{2,14},{3,15},{4,8},{5,9},{6,10},{7,11},{8,4},{9,5},... | collective-permute-start | bytes 73736 | tf_op jit(solution)/shard_map/ppermute | solution.py:263
  40.3 29.1 %collective-permute-start.1 = (bf16[2,128,768]{2,1,0:T(8,128)(2,1)S(1)}, bf16[2,128,768]{2,1,0:T(8,128)(2,1)S(1)}, u32[]{:S(2)}, u32[]{:S(2)}) collective-permute-start(bf16[2,128,768]{2,1,0:T(8,128)(2,1)S(1)} %get-tuple-element.28.own_ref), channel_id=1, source_target_pairs={{0,16},{16,0},{32,48},{48,32},{64,80},{80,64},{96,112},{112,96},{1... | collective-permute-start | bytes 1179656 | tf_op jit(solution)/shard_map/ppermute | solution.py:263
  44.1 17.4 %collective-permute-start.12 = (bf16[3,128,128]{2,1,0:T(8,128)(2,1)S(1)}, bf16[3,128,128]{2,1,0:T(8,128)(2,1)S(1)}, u32[]{:S(2)}, u32[]{:S(2)}) collective-permute-start(bf16[3,128,128]{2,1,0:T(8,128)(2,1)S(1)} %constant_dynamic-update-slice_fusion.kv0_ref), channel_id=1, source_target_pairs={{0,1},{1,0},{2,3},{3,2},{4,5},{5,4},{6,7},{7,6},{8,9},{9,8},{10,11... | collective-permute-start | bytes 294920 | tf_op jit(solution)/shard_map/ppermute | solution.py:263
  45.3 16.2 %collective-permute-start.13 = (bf16[3,128,128]{2,1,0:T(8,128)(2,1)S(1)}, bf16[3,128,128]{2,1,0:T(8,128)(2,1)S(1)}, u32[]{:S(2)}, u32[]{:S(2)}) collective-permute-start(bf16[3,128,128]{2,1,0:T(8,128)(2,1)S(1)} %constant_dynamic-update-slice_fusion.kv0_ref), channel_id=1, source_target_pairs={{0,2},{1,3},{2,0},{3,1},{4,6},{5,7},{6,4},{7,5},{8,10},{9,11},{10,... | collective-permute-start | bytes 294920 | tf_op jit(solution)/shard_map/ppermute | solution.py:263
  47.7 13.7 %collective-permute-start.14 = (bf16[3,128,128]{2,1,0:T(8,128)(2,1)S(1)}, bf16[3,128,128]{2,1,0:T(8,128)(2,1)S(1)}, u32[]{:S(2)}, u32[]{:S(2)}) collective-permute-start(bf16[3,128,128]{2,1,0:T(8,128)(2,1)S(1)} %constant_dynamic-update-slice_fusion.kv0_ref), channel_id=1, source_target_pairs={{0,3},{1,2},{2,1},{3,0},{4,7},{5,6},{6,5},{7,4},{8,11},{9,10},{10,... | collective-permute-start | bytes 294920 | tf_op jit(solution)/shard_map/ppermute | solution.py:263
  47.9 21.5 %collective-permute-start.2 = (bf16[2,128,768]{2,1,0:T(8,128)(2,1)S(1)}, bf16[2,128,768]{2,1,0:T(8,128)(2,1)S(1)}, u32[]{:S(2)}, u32[]{:S(2)}) collective-permute-start(bf16[2,128,768]{2,1,0:T(8,128)(2,1)S(1)} %collective-permute-done.r1_ref), channel_id=1, source_target_pairs={{0,16},{16,0},{32,48},{48,32},{64,80},{80,64},{96,112},{112,96},{1... | collective-permute-start | bytes 1179656 | tf_op jit(solution)/shard_map/ppermute | solution.py:263
  63.9 16.1 %collective-permute-start.18 = (f32[3,32,128]{2,1,0:T(8,128)S(1)}, f32[3,32,128]{2,1,0:T(8,128)S(1)}, u32[]{:S(2)}, u32[]{:S(2)}) collective-permute-start(f32[3,32,128]{2,1,0:T(8,128)S(1)} %get-tuple-element.45), channel_id=1, source_target_pairs={{0,16},{16,0},{32,48},{48,32},{64,80},{80,64},{96,112},{112,96},{1... | collective-permute-start | bytes 147464 | tf_op jit(solution)/shard_map/ppermute | solution.py:263
  63.9 16.2 %collective-permute-start.19 = (f32[3,32,128]{2,1,0:T(8,128)S(1)}, f32[3,32,128]{2,1,0:T(8,128)S(1)}, u32[]{:S(2)}, u32[]{:S(2)}) collective-permute-start(f32[3,32,128]{2,1,0:T(8,128)S(1)} %get-tuple-element.46), channel_id=1, source_target_pairs={{0,32},{16,48},{32,0},{48,16},{64,96},{80,112},{96,64},{112,80},{1... | collective-permute-start | bytes 147464 | tf_op jit(solution)/shard_map/ppermute | solution.py:263
  64.3 15.7 %collective-permute-start.20 = (f32[3,32,128]{2,1,0:T(8,128)S(1)}, f32[3,32,128]{2,1,0:T(8,128)S(1)}, u32[]{:S(2)}, u32[]{:S(2)}) collective-permute-start(f32[3,32,128]{2,1,0:T(8,128)S(1)} %get-tuple-element.47), channel_id=1, source_target_pairs={{0,48},{16,32},{32,16},{48,0},{64,112},{80,96},{96,80},{112,64},{1... | collective-permute-start | bytes 147464 | tf_op jit(solution)/shard_map/ppermute | solution.py:263
  66.0 14.0 %all-to-all-start = ((f32[16,8,128]{2,1,0:T(8,128)}), f32[16,8,128]{2,1,0:T(8,128)S(1)}, u32[]{:S(2)}, u32[]{:S(2)}) async-start(f32[16,8,128]{2,1,0:T(8,128)} %get-tuple-element.48), calls=%async_computation | async-start | bytes 131072 | tf_op jit(solution)/shard_map/all_to_all | solution.py:320
  71.2 1.4 %copy-start.5 = (f32[512,768]{1,0:T(8,128)S(1)}, f32[512,768]{1,0:T(8,128)}, u32[]{:S(2)}) copy-start(f32[512,768]{1,0:T(8,128)} %copy-done.4) | copy-start | bytes 4718596
  (6 other events, 6.6 us)
where the time goes:
time: 83.2 us; the launch traced here: 82.9 us
  starting transfers between devices  37.1 us (45%)
  Pallas kernels  25.3 us (30%)
  waiting for transfers between devices  10.7 us (13%)
  local copies, waits for them, and re-layouts  9.43 us (11%)
    ppermute x21, starting transfers between devices, permute(): lax.ppermute(x, axis, [(i, partner(i)) for i in range(lax.axis_size(axis))])  33.7 us
    pallas_call x8, Pallas kernels, run(): pl.pallas_call(kernel, out_shape=[jax.ShapeDtypeStruct(s, d) for s, d in...  25.3 us
    ppermute x21, waiting for transfers between devices, permute(): lax.ppermute(x, axis, [(i, partner(i)) for i in range(lax.axis_size(axis))])  10.7 us
    unnamed x19, local copies, waits for them, and re-layouts  9.42 us
    all_to_all x1, starting transfers between devices, per_device(): fifth = lax.all_to_all(fifth, ('gx', 'gy'), 0, 0, axis_index_groups=groups)  3.39 us
  transfers between devices with their start and end apart: 22, of which 2 were waited for; matrix products, arithmetic and copies ran while one was open for 0% of the time, Pallas kernels for 26%

commit v1 on v0

v1 whole, which is shorter than its diff:
```python
import functools

import jax
import jax.numpy as jnp
from jax import lax
from jax.experimental import pallas as pl
from jax.experimental.pallas import tpu as pltpu
from jax.sharding import PartitionSpec as P

HEADS = 12
HEAD = 64
WIDTH = 768
ROWS = 512
LOG2E = 1.4426950408889634
SCALE = LOG2E / 8.0
LOW = -3.0e38
BF = jnp.bfloat16
F32 = jnp.float32


def dot(a, b):
    return lax.dot_general(a, b, (((1,), (0,)), ((), ())), preferred_element_type=F32)


def dot_t(a, b):
    return lax.dot_general(a, b, (((1,), (1,)), ((), ())), preferred_element_type=F32)


def softmax_parts(scores):
    top = jnp.max(scores, axis=-1, keepdims=True)
    expo = jnp.exp2((scores - top) * SCALE)
    total = jnp.sum(expo, axis=-1, keepdims=True)
    return expo.astype(BF), 1.0 / total, top * SCALE + jnp.log(total) * LOG2E


def lanes(shape):
    return lax.broadcasted_iota(jnp.int32, shape, len(shape) - 1)


def sorted_position(index):
    return (
        (index >> 7)
        + 4 * ((index >> 5) & 3)
        + 16 * ((index >> 3) & 3)
        + 64 * ((index >> 1) & 3)
        + 256 * (index & 1)
    )


def small_pick_kernel(t_ref, q_ref, kv_ref, own_ref, one_ref, two_ref, three_ref, chunks):
    row = lax.broadcasted_iota(jnp.int32, (64, ROWS), 0)
    col = lax.broadcasted_iota(jnp.int32, (64, ROWS), 1)
    j = row & 31
    base = (row >> 5) + 16 * (j >> 3) + 64 * ((j >> 1) & 3) + 256 * (j & 1)
    zeros = jnp.zeros((32, HEAD), F32)
    for pair in range(HEADS // 2):
        onehot = (col == base + 2 * pair).astype(F32).astype(BF)
        cols = pl.ds(pair * 128, 128)
        q = dot(onehot, q_ref[0, :, cols])
        k = dot(onehot, kv_ref[0, 0, :, cols])
        v = dot(onehot, kv_ref[1, 0, :, cols])
        for side in range(2):
            head = 2 * pair + side
            rs = slice(side * 32, side * 32 + 32)
            cs = slice(side * HEAD, side * HEAD + HEAD)
            t, i = head // 3, head % 3
            chunks[t, i, 0] = jnp.concatenate([k[rs, cs], v[rs, cs]], axis=1).astype(BF)
            chunks[t, i, 1] = jnp.concatenate([q[rs, cs], zeros], axis=1).astype(BF)
    t = t_ref[0]
    own_ref[...] = chunks[t]
    one_ref[...] = chunks[t ^ 1]
    two_ref[...] = chunks[t ^ 2]
    three_ref[...] = chunks[t ^ 3]


def sort_kernel(q_ref, kv_ref, qs_ref, ks_ref, vs_ref, send_ref):
    row = lax.broadcasted_iota(jnp.int32, (ROWS, ROWS), 0)
    col = lax.broadcasted_iota(jnp.int32, (ROWS, ROWS), 1)
    onehot = (col == sorted_position(row)).astype(F32).astype(BF)
    half = lanes((128, 128)) < HEAD
    for pair in range(HEADS // 2):
        cols = pl.ds(pair * 128, 128)
        a, b = (2 * pair) % 4 * 128, (2 * pair + 1) % 4 * 128
        qs_ref[:, cols] = dot(onehot, q_ref[0, :, cols]).astype(BF)
        for n, ref in ((0, ks_ref), (1, vs_ref)):
            x = dot(onehot, kv_ref[n, 0, :, cols])
            ref[:, cols] = x.astype(BF)
            send_ref[n, :, cols] = jnp.where(half, x[a : a + 128], x[b : b + 128]).astype(BF)


def attend_pair(q, k, v):
    n = q.shape[0]
    half = lanes(q.shape) < HEAD
    zero = jnp.zeros((), BF)
    stacked = jnp.concatenate([jnp.where(half, q, zero), jnp.where(half, zero, q)], axis=0)
    p, inv, log = softmax_parts(dot_t(stacked, k))
    return dot(p, v) * inv, log, n


def level1_kernel(first, q_ref, k_ref, v_ref, *rest):
    a_ref, oe_ref, q2_ref = rest[-3:]
    half = lanes((256, 128)) < HEAD
    for pair in (first, first + 1):
        cols = slice(pair * 128, pair * 128 + 128)
        k, v = k_ref[:, cols], v_ref[:, cols]
        for c in range(2):
            rows = slice(c * 256, c * 256 + 256)
            q = q_ref[rows, cols]
            out, log, n = attend_pair(q, k, v)
            a_ref[rows, cols] = jnp.where(half, out[:n], out[n:]).astype(BF)
            if c == pair % 2:
                oe_ref[0, :, cols] = jnp.where(half[:128], out[:128], out[n + 128 :])
                oe_ref[1, :, cols] = jnp.where(half[:128], log[:128], log[n + 128 :])
                q2_ref[:, cols] = jnp.where(half[:128], q[:128], q[128:])


def level2_kernel(q_ref, own_ref, r1_ref, r2_ref, r3_ref, oe_ref, a_ref, o_ref, e_ref):
    half = lanes((128, 128)) < HEAD
    refs = (own_ref, r1_ref, r2_ref, r3_ref)
    for pair in range(HEADS // 2):
        cols = slice(pair * 128, pair * 128 + 128)
        k = jnp.concatenate([r[0, :, cols] for r in refs], axis=0)
        v = jnp.concatenate([r[1, :, cols] for r in refs], axis=0)
        out, log, n = attend_pair(q_ref[:, cols], k, v)
        o, e = mix(
            oe_ref[0, :, cols], oe_ref[1, :, cols],
            jnp.where(half, out[:n], out[n:]), jnp.where(half, log[:n], log[n:]),
        )
        a_ref[:, cols] = o.astype(BF)
        low = pair // 2 * 32
        o_ref[:, cols] = o[low : low + 32]
        e_ref[:, cols] = e[low : low + 32]


def regroup4_kernel(own_ref, r1_ref, r2_ref, r3_ref, kv4_ref, q4_ref):
    refs = (own_ref, r1_ref, r2_ref, r3_ref)
    for i in range(3):
        kv4_ref[i] = jnp.concatenate([r[i, 0].astype(F32)[:8] for r in refs], axis=0).astype(BF)
        q4_ref[i] = jnp.concatenate([r[i, 1].astype(F32)[:8] for r in refs], axis=0).astype(BF)


def regroup3_kernel(own_ref, r1_ref, r2_ref, r3_ref, _, kv_ref, q_ref):
    for i in range(3):
        for n, r in enumerate((own_ref, r1_ref, r2_ref, r3_ref)):
            kv_ref[i, n * 32 : n * 32 + 32, :] = r[i, 0]
            q_ref[i, n * 32 : n * 32 + 32, :] = r[i, 1]


def join_kernel(a_ref, b_ref, *rest):
    out_ref = rest[-1]
    n = a_ref.shape[1]
    for i in range(3):
        out_ref[i, :n] = a_ref[i]
        out_ref[i, n:] = b_ref[i]


def gate_kernel(a_ref, token_ref, out_ref):
    pass


def mix(o1, e1, o2, e2):
    top = jnp.maximum(e1, e2)
    w1, w2 = jnp.exp2(e1 - top), jnp.exp2(e2 - top)
    den = w1 + w2
    return (w1 * o1 + w2 * o2) / den, top + jnp.log(den) * LOG2E


def level5_kernel(t_ref, q0_ref, q1_ref, kv0_ref, kv1_ref, fifth_ref):
    t, y = t_ref[0], t_ref[1]
    half = lanes((128, 128)) < HEAD
    in_five = (lanes((128, 512)) & 7) < 2
    fifth_ref[...] = jnp.zeros_like(fifth_ref)
    for i in range(3):
        kv = jnp.concatenate([kv0_ref[i], kv1_ref[i]], axis=0)
        q = jnp.concatenate([q0_ref[i], q1_ref[i]], axis=0)
        p, inv, log5 = softmax_parts(jnp.where(in_five, dot_t(q, kv), LOW))
        out5 = dot(p, kv) * inv
        both = jnp.where(half, log5, out5)
        for m, apart in enumerate((0, 1, 3, 2)):
            for n in range(4):
                slot = (t ^ n) * 4 + (y ^ apart)
                fifth_ref[slot, 2 * i : 2 * i + 2, :] = both[m * 32 + n * 8 : m * 32 + n * 8 + 2]


def level34_kernel(q_ref, three0_ref, three1_ref, q4_ref, four0_ref, four1_ref, _, *outs):
    half = lanes((128, 128)) < HEAD
    for i in range(3):
        both = []
        for q, kvs in ((q_ref[i], (three0_ref[i], three1_ref[i])), (q4_ref[i], (four0_ref[i], four1_ref[i]))):
            kv = jnp.concatenate(kvs, axis=0)
            p, inv, log = softmax_parts(dot_t(q, kv))
            both.append((dot(p, kv) * inv, log))
        (out3, log3), (out4, log4) = both
        plain = jnp.where(half, log3, out3)
        for n in range(4):
            rs, r3 = slice(n * 8, n * 8 + 8), slice(n * 32, n * 32 + 8)
            o, e = mix(out3[r3], log3[r3], out4[rs], log4[rs])
            outs[n][i, :8, :] = jnp.where(half[:8], e, o)
            outs[n][i, 8:, :] = plain[n * 32 + 8 : n * 32 + 32]


def final_kernel(
    t_ref, a_ref, second_ref, o_ref, e_ref, own_ref, one_ref, two_ref, three_ref, fifth_ref,
    out_ref, rows_ref, back,
):
    t = t_ref[0]
    for n, r in enumerate((own_ref, one_ref, two_ref, three_ref)):
        back[n] = r[...]
    half = lanes((128, 128)) < HEAD
    rows_ref[...] = a_ref[...]
    for pair in range(HEADS // 2):
        cols = slice(pair * 128, pair * 128 + 128)
        second = second_ref[:, cols]
        for side in range(2):
            mine = half if side == 0 else jnp.logical_not(half)
            start = (2 * pair + side) % 4 * 128
            rows = slice(start, start + 128)
            rows_ref[rows, cols] = jnp.where(mine, second, rows_ref[rows, cols])
    for head in range(HEADS):
        source, i = head // 3, head % 3
        got = back[t ^ source, i]
        pieces = [fifth_ref[source * 4 + m, 2 * i : 2 * i + 2, :] for m in range(4)]
        e, o = got[:, :HEAD], got[:, HEAD:]
        e2, o2 = e[:2], o[:2]
        logs = [x[:, :HEAD] for x in pieces]
        top = functools.reduce(jnp.maximum, logs, e2)
        w = [jnp.exp2(x - top) for x in logs]
        w2 = jnp.exp2(e2 - top)
        den = sum(w, w2)
        num = sum((wi * x[:, HEAD:] for wi, x in zip(w, pieces)), w2 * o2)
        o = jnp.concatenate([num / den, o[2:]], axis=0)
        e = jnp.concatenate([top + jnp.log(den) * LOG2E, e[2:]], axis=0)
        cols = slice(head * HEAD, head * HEAD + HEAD)
        mixed, _ = mix(o_ref[:, cols], e_ref[:, cols], o, e)
        base = head % 4 * 128 + head // 4 * 32
        rows_ref[base : base + 32, cols] = mixed.astype(BF)
    row = lax.broadcasted_iota(jnp.int32, (ROWS, ROWS), 0)
    col = lax.broadcasted_iota(jnp.int32, (ROWS, ROWS), 1)
    onehot = (row == sorted_position(col)).astype(F32).astype(BF)
    for pair in range(HEADS // 2):
        cols = pl.ds(pair * 128, 128)
        out_ref[0, :, cols] = dot(onehot, rows_ref[:, cols]).astype(BF)


VMEM = pl.BlockSpec(memory_space=pltpu.VMEM)
ANY = pl.BlockSpec(memory_space=pl.ANY)
SMEM = pl.BlockSpec(memory_space=pltpu.SMEM)


def call(kernel, outs, in_specs=None, scratch=(), flops=0, nbytes=0, limit=24, **more):
    def run(*args):
        specs = in_specs if in_specs is not None else [VMEM] * len(args)
        out_specs = more.pop("out_specs", None) or [VMEM] * len(outs)
        return pl.pallas_call(
            kernel,
            out_shape=[jax.ShapeDtypeStruct(s, d) for s, d in outs],
            in_specs=specs,
            out_specs=out_specs,
            scratch_shapes=list(scratch),
            cost_estimate=pl.CostEstimate(flops=flops, bytes_accessed=nbytes, transcendentals=0),
            compiler_params=pltpu.CompilerParams(vmem_limit_bytes=limit << 20),
            **more,
        )(*args)

    return run


def permute(x, axis, partner):
    return lax.ppermute(x, axis, [(i, partner(i)) for i in range(lax.axis_size(axis))])


def per_device(queries, key_values):
    gx, gy = lax.axis_index("gx"), lax.axis_index("gy")
    place = jnp.stack([gx & 3, gy >> 2]).astype(jnp.int32)

    chunk = ((3, 2, 32, 128), BF)
    own, c1, c2, c3 = call(
        small_pick_kernel, [chunk] * 4, [SMEM, VMEM, VMEM], [pltpu.VMEM((4, 3, 2, 32, 128), BF)],
        nbytes=3 << 20,
    )(place, queries, key_values)
    g = [own] + [permute(c, "gx", lambda i, n=n: i ^ n) for n, c in ((1, c1), (2, c2), (3, c3))]

    qs, ks, vs, send2 = call(
        sort_kernel, [((ROWS, WIDTH), BF)] * 3 + [((2, 128, WIDTH), BF)], nbytes=6 << 20
    )(queries, key_values)

    def level1(n, *tokens, held=()):
        return call(
            functools.partial(level1_kernel, 2 * n),
            [((ROWS, WIDTH), BF), ((2, 128, WIDTH), F32), ((128, WIDTH), BF)],
            [VMEM] * 3 + [ANY] * len(tokens) + [VMEM] * len(held), flops=1 << 31, nbytes=2 << 20,
            input_output_aliases={3 + len(tokens) + i: i for i in range(len(held))},
        )(qs, ks, vs, *tokens, *held)

    def join(a, b, *tokens):
        shape = (a.shape[0], 2 * a.shape[1], a.shape[2])
        return call(join_kernel, [(shape, BF)], [VMEM] * 2 + [ANY] * len(tokens), nbytes=1 << 18, limit=4)(
            a, b, *tokens
        )[0]

    def gate(x, token):
        return call(
            gate_kernel, [(x.shape, x.dtype)], [ANY, ANY], out_specs=[ANY], input_output_aliases={0: 0}, limit=4
        )(x, token)[0]

    kv4, q4 = call(regroup4_kernel, [((3, 32, 128), BF)] * 2, nbytes=1 << 19, limit=4)(*g)
    z4 = permute(kv4, "gx", lambda i: i ^ 4)
    y5 = permute(q4, "gy", lambda i: i ^ 4)
    held = level1(0, kv4)
    kv4 = join(kv4, z4, held[2])
    z4 = permute(kv4, "gx", lambda i: i ^ 12)
    kv3, q3 = call(regroup3_kernel, [((3, 128, 128), BF)] * 2, [VMEM] * 4 + [ANY], nbytes=1 << 19, limit=4)(
        *g, kv4
    )
    z3 = permute(kv3, "gx", lambda i: i ^ 4)
    q5 = join(q4, y5, kv4)
    y5 = permute(q5, "gy", lambda i: i ^ 12)
    held = level1(1, kv3, q5, held=held)
    kv4 = join(kv4, z4, held[2])
    x4 = permute(kv4, "gy", lambda i: i ^ 1)
    kv3 = join(kv3, z3, kv4)
    z3 = permute(kv3, "gx", lambda i: i ^ 12)
    held = level1(2, kv3, y5, held=held)
    kv4 = join(kv4, x4, held[2])
    x4 = permute(kv4, "gy", lambda i: i ^ 3)
    send2 = gate(send2, kv4)
    far2 = permute(send2, "gx", lambda i: i ^ 2)
    near2 = permute(send2, "gx", lambda i: i ^ 1)
    (fifth,) = call(level5_kernel, [((16, 8, 128), F32)], [SMEM] + [VMEM] * 4, nbytes=1 << 20)(
        place, q5, y5, kv4, x4
    )
    groups = [
        [(4 * zg + t) * 16 + (4 * y + x) for t in range(4) for y in range(4)]
        for zg in range(4)
        for x in range(4)
    ]
    spread = lax.all_to_all(fifth, ("gx", "gy"), 0, 0, axis_index_groups=groups)
    part = ((3, 32, 128), F32)
    p0, p1, p2, p3 = call(level34_kernel, [part] * 4, [VMEM] * 6 + [ANY], nbytes=1 << 20)(
        q3, kv3, z3, q4, kv4, x4, fifth
    )
    far2 = gate(far2, p0)
    other2 = permute(far2, "gx", lambda i: i ^ 1)
    second, o12, e12 = call(
        level2_kernel, [((128, WIDTH), BF), ((32, WIDTH), F32), ((32, WIDTH), F32)],
        flops=1 << 31, nbytes=3 << 20,
    )(held[2], send2, far2, near2, other2, held[1])
    back = [p0] + [permute(x, "gx", lambda i, n=n: i ^ n) for n, x in ((1, p1), (2, p2), (3, p3))]
    (out,) = call(
        final_kernel, [((1, ROWS, WIDTH), BF)], [SMEM] + [VMEM] * 9,
        [pltpu.VMEM((ROWS, WIDTH), BF), pltpu.VMEM((4, 3, 32, 128), F32)], nbytes=4 << 20,
    )(place, held[0], second, o12, e12, *back, spread)
    return out


def solution(mesh):
    return jax.shard_map(
        per_device,
        mesh=mesh,
        in_specs=(P("gy", "gx", None), P(None, "gy", "gx", None)),
        out_specs=P("gy", "gx", None),
        check_vma=False,
    )
```

time: 83.2 us -> 60.1 us (0.72)
  Pallas kernels: 25.3 us -> 17.6 us
  waiting for transfers between devices: 10.7 us -> 3.65 us
  local copies, waits for them, and re-layouts: 9.43 us -> 3.76 us
  starting transfers between devices: 37.1 us -> 34.6 us
    pallas_call x8 -> x18, Pallas kernels: 25.3 us -> 17.6 us  [run(): pl.pallas_call(kernel, out_shape=[jax.ShapeDtypeStruct(s, d) for s, d in...]
    ppermute x21 -> x17, waiting for transfers between devices: 10.7 us -> 3.64 us  [permute(): lax.ppermute(x, axis, [(i, partner(i)) for i in range(lax.axis_size(axis))])]
    unnamed x19 -> x8, local copies, waits for them, and re-layouts: 9.42 us -> 3.76 us
    ppermute x21 -> x17, starting transfers between devices: 33.7 us -> 30.3 us  [permute(): lax.ppermute(x, axis, [(i, partner(i)) for i in range(lax.axis_size(axis))])]
    all_to_all x1, starting transfers between devices: 3.39 us -> 4.27 us  [per_device(): spread = lax.all_to_all(fifth, ('gx', 'gy'), 0, 0, axis_index_groups=groups)]
  transfers between devices with their start and end apart: 22 -> 18, of which waited for: 2 -> 4; matrix products, arithmetic and copies ran while one was open for 0% -> 0% of each run, Pallas kernels for 26% -> 23%
where the time goes in v1:
time: 60.1 us; the launch traced here: 59.9 us
  starting transfers between devices  34.6 us (58%)
  Pallas kernels  17.6 us (29%)
  local copies, waits for them, and re-layouts  3.76 us (6%)
  waiting for transfers between devices  3.65 us (6%)
    ppermute x17, starting transfers between devices, permute(): lax.ppermute(x, axis, [(i, partner(i)) for i in range(lax.axis_size(axis))])  30.3 us
    pallas_call x18, Pallas kernels, run(): pl.pallas_call(kernel, out_shape=[jax.ShapeDtypeStruct(s, d) for s, d in...  17.6 us
    all_to_all x1, starting transfers between devices, per_device(): spread = lax.all_to_all(fifth, ('gx', 'gy'), 0, 0, axis_index_groups=groups)  4.27 us
    unnamed x8, local copies, waits for them, and re-layouts  3.76 us
    ppermute x17, waiting for transfers between devices, permute(): lax.ppermute(x, axis, [(i, partner(i)) for i in range(lax.axis_size(axis))])  3.64 us
  transfers between devices with their start and end apart: 18, of which 4 were waited for; matrix products, arithmetic and copies ran while one was open for 0% of the time, Pallas kernels for 23%

profile of v1, /device:TPU:1, one launch (start us, length us, event | category | flops | bytes accessed | tf_op | source)
XLA Modules:
  0.0 59.9 jit_solution(13549754854785550464)
XLA Ops:
  0.1 1.4 %copy-done = bf16[2,1,512,768]{3,2,1,0:T(8,128)(2,1)S(1)} copy-done((bf16[2,1,512,768]{3,2,1,0:T(8,128)(2,1)S(1)}, bf16[2,1,512,768]{3,2,1,0:T(8,128)(2,1)}, u32[]{:S(2)}) %copy-start) | copy-done | bytes 1572888
  1.5 1.1 %copy-done.1 = bf16[1,512,768]{2,1,0:T(8,128)(2,1)S(1)} copy-done((bf16[1,512,768]{2,1,0:T(8,128)(2,1)S(1)}, bf16[1,512,768]{2,1,0:T(8,128)(2,1)}, u32[]{:S(2)}) %copy-start.1) | copy-done | bytes 786456
  3.7 3.3 %collective-permute-start = (bf16[3,2,32,128]{3,2,1,0:T(8,128)(2,1)S(1)}, bf16[3,2,32,128]{3,2,1,0:T(8,128)(2,1)S(1)}, u32[]{:S(2)}, u32[]{:S(2)}) collective-permute-start(bf16[3,2,32,128]{3,2,1,0:T(8,128)(2,1)S(1)} %get-tuple-element.37), channel_id=1, source_target_pairs={{0,16},{16,0},{32,48},{48,32},{64,80},{80,64},{96,112},{112,96},{1... | collective-permute-start | bytes 147464 | tf_op jit(solution)/shard_map/ppermute | solution.py:269
  7.1 1.7 %collective-permute-start.2 = (bf16[3,2,32,128]{3,2,1,0:T(8,128)(2,1)S(1)}, bf16[3,2,32,128]{3,2,1,0:T(8,128)(2,1)S(1)}, u32[]{:S(2)}, u32[]{:S(2)}) collective-permute-start(bf16[3,2,32,128]{3,2,1,0:T(8,128)(2,1)S(1)} %get-tuple-element.39), channel_id=1, source_target_pairs={{0,48},{16,32},{32,16},{48,0},{64,112},{80,96},{96,80},{112,64},{1... | collective-permute-start | bytes 147464 | tf_op jit(solution)/shard_map/ppermute | solution.py:269
  8.8 2.7 %shard_map.28 = (bf16[512,768]{1,0:T(8,128)(2,1)S(1)}, bf16[512,768]{1,0:T(8,128)(2,1)S(1)}, bf16[512,768]{1,0:T(8,128)(2,1)S(1)}, bf16[2,128,768]{2,1,0:T(8,128)(2,1)S(1)}) custom-call(bf16[1,512,768]{2,1,0:T(8,128)(2,1)S(1)} %copy-done.1, bf16[2,1,512,768]{3,2,1,0:T(8,128)(2,1)S(1)} %copy-done), custom_call_target="tpu_custom_call" | custom-call | bytes 6291456 | tf_op jit(solution)/shard_map/pallas_call | solution.py:254
  11.6 2.2 %collective-permute-start.3 = (bf16[3,32,128]{2,1,0:T(8,128)(2,1)S(1)}, bf16[3,32,128]{2,1,0:T(8,128)(2,1)S(1)}, u32[]{:S(2)}, u32[]{:S(2)}) collective-permute-start(bf16[3,32,128]{2,1,0:T(8,128)(2,1)S(1)} %get-tuple-element.40.rest_0_.a_ref), channel_id=1, source_target_pairs={{0,64},{16,80},{32,96},{48,112},{64,0},{80,16},{96,32},{112,48},{1... | collective-permute-start | bytes 73736 | tf_op jit(solution)/shard_map/ppermute | solution.py:269
  13.8 1.3 %collective-permute-start.6 = (bf16[3,32,128]{2,1,0:T(8,128)(2,1)S(1)}, bf16[3,32,128]{2,1,0:T(8,128)(2,1)S(1)}, u32[]{:S(2)}, u32[]{:S(2)}) collective-permute-start(bf16[3,32,128]{2,1,0:T(8,128)(2,1)S(1)} %get-tuple-element.43.a_ref.q4_ref), channel_id=1, source_target_pairs={{0,4},{1,5},{2,6},{3,7},{4,0},{5,1},{6,2},{7,3},{8,12},{9,13},{10,... | collective-permute-start | bytes 73736 | tf_op jit(solution)/shard_map/ppermute | solution.py:269
  15.1 1.7 %shard_map.31 = (bf16[512,768]{1,0:T(8,128)(2,1)S(1)}, f32[2,128,768]{2,1,0:T(8,128)S(1)}, bf16[128,768]{1,0:T(8,128)(2,1)S(1)}) custom-call(bf16[512,768]{1,0:T(8,128)(2,1)S(1)} %get-tuple-element.33.q_ref, bf16[512,768]{1,0:T(8,128)(2,1)S(1)} %get-tuple-element.34.k_ref, bf16[512,768]{1,0:T(8,128)(2,1)S(1)} %get-tuple-element.35.v_ref, ...), custom_call_target="tpu_custom_call" | custom-call | flops 2147483648 | bytes 2097152 | tf_op jit(solution)/shard_map/pallas_call | solution.py:254
  16.8 3.5 %collective-permute-start.5 = (bf16[3,64,128]{2,1,0:T(8,128)(2,1)S(1)}, bf16[3,64,128]{2,1,0:T(8,128)(2,1)S(1)}, u32[]{:S(2)}, u32[]{:S(2)}) collective-permute-start(bf16[3,64,128]{2,1,0:T(8,128)(2,1)S(1)} %shard_map.32._.rest_0_.a_ref), channel_id=1, source_target_pairs={{0,192},{16,208},{32,224},{48,240},{64,128},{80,144},{96,160},{112... | collective-permute-start | bytes 147464 | tf_op jit(solution)/shard_map/ppermute | solution.py:269
  20.3 1.3 %collective-permute-start.4 = (bf16[3,128,128]{2,1,0:T(8,128)(2,1)S(1)}, bf16[3,128,128]{2,1,0:T(8,128)(2,1)S(1)}, u32[]{:S(2)}, u32[]{:S(2)}) collective-permute-start(bf16[3,128,128]{2,1,0:T(8,128)(2,1)S(1)} %get-tuple-element.42.rest_0_.a_ref), channel_id=1, source_target_pairs={{0,64},{16,80},{32,96},{48,112},{64,0},{80,16},{96,32},{112,48},{1... | collective-permute-start | bytes 294920 | tf_op jit(solution)/shard_map/ppermute | solution.py:269
  21.6 2.1 %collective-permute-start.7 = (bf16[3,64,128]{2,1,0:T(8,128)(2,1)S(1)}, bf16[3,64,128]{2,1,0:T(8,128)(2,1)S(1)}, u32[]{:S(2)}, u32[]{:S(2)}) collective-permute-start(bf16[3,64,128]{2,1,0:T(8,128)(2,1)S(1)} %shard_map.34.rest_1_.q0_ref), channel_id=1, source_target_pairs={{0,12},{1,13},{2,14},{3,15},{4,8},{5,9},{6,10},{7,11},{8,4},{9,5},... | collective-permute-start | bytes 147464 | tf_op jit(solution)/shard_map/ppermute | solution.py:269
  23.7 1.7 %shard_map.35 = (bf16[512,768]{1,0:T(8,128)(2,1)S(1)}, f32[2,128,768]{2,1,0:T(8,128)S(1)}, bf16[128,768]{1,0:T(8,128)(2,1)S(1)}) custom-call(bf16[512,768]{1,0:T(8,128)(2,1)S(1)} %get-tuple-element.33.q_ref, bf16[512,768]{1,0:T(8,128)(2,1)S(1)} %get-tuple-element.34.k_ref, ...), custom_call_target="tpu_custom_call", output_to_operand_aliasing={{0}: (5, {}), {1}: (6, {}), {2}: (7, {})} | custom-call | flops 2147483648 | bytes 2097152 | tf_op jit(solution)/shard_map/pallas_call | solution.py:254
  25.4 1.5 %collective-permute-start.8 = (bf16[3,128,128]{2,1,0:T(8,128)(2,1)S(1)}, bf16[3,128,128]{2,1,0:T(8,128)(2,1)S(1)}, u32[]{:S(2)}, u32[]{:S(2)}) collective-permute-start(bf16[3,128,128]{2,1,0:T(8,128)(2,1)S(1)} %shard_map.36.rest_0_.a_ref), channel_id=1, source_target_pairs={{0,1},{1,0},{2,3},{3,2},{4,5},{5,4},{6,7},{7,6},{8,9},{9,8},{10,11... | collective-permute-start | bytes 294920 | tf_op jit(solution)/shard_map/ppermute | solution.py:269
  27.5 1.7 %shard_map.38 = (bf16[512,768]{1,0:T(8,128)(2,1)S(1)}, f32[2,128,768]{2,1,0:T(8,128)S(1)}, bf16[128,768]{1,0:T(8,128)(2,1)S(1)}) custom-call(bf16[512,768]{1,0:T(8,128)(2,1)S(1)} %get-tuple-element.33.q_ref, bf16[512,768]{1,0:T(8,128)(2,1)S(1)} %get-tuple-element.34.k_ref, ...), custom_call_target="tpu_custom_call", output_to_operand_aliasing={{0}: (5, {}), {1}: (6, {}), {2}: (7, {})} | custom-call | flops 2147483648 | bytes 2097152 | tf_op jit(solution)/shard_map/pallas_call | solution.py:254
  30.1 2.5 %collective-permute-start.11 = (bf16[3,256,128]{2,1,0:T(8,128)(2,1)S(1)}, bf16[3,256,128]{2,1,0:T(8,128)(2,1)S(1)}, u32[]{:S(2)}, u32[]{:S(2)}) collective-permute-start(bf16[3,256,128]{2,1,0:T(8,128)(2,1)S(1)} %shard_map.39.token_ref.kv0_ref.four0_ref), channel_id=1, source_target_pairs={{0,3},{1,2},{2,1},{3,0},{4,7},{5,6},{6,5},{7,4},{8,11},{9,10},{10,... | collective-permute-start | bytes 589832 | tf_op jit(solution)/shard_map/ppermute | solution.py:269
  32.9 4.2 %collective-permute-start.12 = (bf16[2,128,768]{2,1,0:T(8,128)(2,1)S(1)}, bf16[2,128,768]{2,1,0:T(8,128)(2,1)S(1)}, u32[]{:S(2)}, u32[]{:S(2)}) collective-permute-start(bf16[2,128,768]{2,1,0:T(8,128)(2,1)S(1)} %shard_map.40.own_ref), channel_id=1, source_target_pairs={{0,16},{16,0},{32,48},{48,32},{64,80},{80,64},{96,112},{112,96},{1... | collective-permute-start | bytes 1179656 | tf_op jit(solution)/shard_map/ppermute | solution.py:269
  37.1 2.1 %shard_map.41._ = f32[16,8,128]{2,1,0:T(8,128)} custom-call(s32[2]{0:T(128)S(1)} %pad_add_fusion.t_ref, bf16[3,64,128]{2,1,0:T(8,128)(2,1)S(1)} %shard_map.34.rest_1_.q0_ref, bf16[3,64,128]{2,1,0:T(8,128)(2,1)S(1)} %collective-permute-done.7.rest_1_.q1_ref, bf16[3,256,128]{2,1,0:T(8,128)(2,1)S(1)} %shard_map.39.token_ref.kv0_ref.four0_ref, ...), custom_call_target="tpu_custom_call" | custom-call | bytes 1048576 | tf_op jit(solution)/shard_map/pallas_call | solution.py:254
  39.2 2.2 %collective-permute-done.10.three1_ref = bf16[3,256,128]{2,1,0:T(8,128)(2,1)S(1)} collective-permute-done((bf16[3,256,128]{2,1,0:T(8,128)(2,1)S(1)}, bf16[3,256,128]{2,1,0:T(8,128)(2,1)S(1)}, u32[]{:S(2)}, u32[]{:S(2)}) %collective-permute-start.10) | collective-permute-done | bytes 196640 | tf_op jit(solution)/shard_map/ppermute | solution.py:269
  41.4 1.7 %shard_map.42 = (f32[3,32,128]{2,1,0:T(8,128)S(1)}, f32[3,32,128]{2,1,0:T(8,128)S(1)}, f32[3,32,128]{2,1,0:T(8,128)S(1)}, f32[3,32,128]{2,1,0:T(8,128)S(1)}) custom-call(bf16[3,128,128]{2,1,0:T(8,128)(2,1)S(1)} %get-tuple-element.52.q_ref, bf16[3,256,128]{2,1,0:T(8,128)(2,1)S(1)} %shard_map.37.rest_0_.three0_ref, ...), custom_call_target="tpu_custom_call" | custom-call | bytes 1048576 | tf_op jit(solution)/shard_map/pallas_call | solution.py:254
  43.1 3.5 %collective-permute-start.13 = (bf16[2,128,768]{2,1,0:T(8,128)(2,1)S(1)}, bf16[2,128,768]{2,1,0:T(8,128)(2,1)S(1)}, u32[]{:S(2)}, u32[]{:S(2)}) collective-permute-start(bf16[2,128,768]{2,1,0:T(8,128)(2,1)S(1)} %shard_map.43.r1_ref), channel_id=1, source_target_pairs={{0,16},{16,0},{32,48},{48,32},{64,80},{80,64},{96,112},{112,96},{1... | collective-permute-start | bytes 1179656 | tf_op jit(solution)/shard_map/ppermute | solution.py:269
  46.6 4.3 %all-to-all-start = ((f32[16,8,128]{2,1,0:T(8,128)}), f32[16,8,128]{2,1,0:T(8,128)S(1)}, u32[]{:S(2)}, u32[]{:S(2)}) async-start(f32[16,8,128]{2,1,0:T(8,128)} %shard_map.41._), calls=%async_computation | async-start | bytes 131072 | tf_op jit(solution)/shard_map/all_to_all | solution.py:337
  51.0 1.7 %collective-permute-start.15 = (f32[3,32,128]{2,1,0:T(8,128)S(1)}, f32[3,32,128]{2,1,0:T(8,128)S(1)}, u32[]{:S(2)}, u32[]{:S(2)}) collective-permute-start(f32[3,32,128]{2,1,0:T(8,128)S(1)} %get-tuple-element.59), channel_id=1, source_target_pairs={{0,32},{16,48},{32,0},{48,16},{64,96},{80,112},{96,64},{112,80},{1... | collective-permute-start | bytes 147464 | tf_op jit(solution)/shard_map/ppermute | solution.py:269
  54.2 2.1 %shard_map.44 = (bf16[128,768]{1,0:T(8,128)(2,1)S(1)}, f32[32,768]{1,0:T(8,128)S(1)}, f32[32,768]{1,0:T(8,128)S(1)}) custom-call(bf16[128,768]{1,0:T(8,128)(2,1)S(1)} %get-tuple-element.50.rest_0_.q_ref, bf16[2,128,768]{2,1,0:T(8,128)(2,1)S(1)} %shard_map.40.own_ref, bf16[2,128,768]{2,1,0:T(8,128)(2,1)S(1)} %shard_map.43.r1_ref, ...), custom_call_target="tpu_custom_call" | custom-call | flops 2147483648 | bytes 3145728 | tf_op jit(solution)/shard_map/pallas_call | solution.py:254
  57.1 2.8 %shard_map.45 = bf16[1,512,768]{2,1,0:T(8,128)(2,1)} custom-call(s32[2]{0:T(128)S(1)} %pad_add_fusion.t_ref, bf16[512,768]{1,0:T(8,128)(2,1)S(1)} %get-tuple-element.49.a_ref, bf16[128,768]{1,0:T(8,128)(2,1)S(1)} %get-tuple-element.55.second_ref, f32[32,768]{1,0:T(8,128)S(1)} %get-tuple-element.56.o_ref, f32[32,768]{1,0:T(8,128)S(1)} %get-tuple-element.57.e_ref, ...), custom_call_target="tpu_custom_call" | custom-call | bytes 4194304 | tf_op jit(solution)/shard_map/pallas_call | solution.py:254
  (39 shorter events, 5.5 us)
Async XLA Ops:
  0.1 1.4 %copy-start = (bf16[2,1,512,768]{3,2,1,0:T(8,128)(2,1)S(1)}, bf16[2,1,512,768]{3,2,1,0:T(8,128)(2,1)}, u32[]{:S(2)}) copy-start(bf16[2,1,512,768]{3,2,1,0:T(8,128)(2,1)} %kv_ref.3) | copy-start | bytes 4718596
  1.5 1.1 %copy-start.1 = (bf16[1,512,768]{2,1,0:T(8,128)(2,1)S(1)}, bf16[1,512,768]{2,1,0:T(8,128)(2,1)}, u32[]{:S(2)}) copy-start(bf16[1,512,768]{2,1,0:T(8,128)(2,1)} %q_ref.3) | copy-start | bytes 2359300
  3.7 7.7 %collective-permute-start = (bf16[3,2,32,128]{3,2,1,0:T(8,128)(2,1)S(1)}, bf16[3,2,32,128]{3,2,1,0:T(8,128)(2,1)S(1)}, u32[]{:S(2)}, u32[]{:S(2)}) collective-permute-start(bf16[3,2,32,128]{3,2,1,0:T(8,128)(2,1)S(1)} %get-tuple-element.37), channel_id=1, source_target_pairs={{0,16},{16,0},{32,48},{48,32},{64,80},{80,64},{96,112},{112,96},{1... | collective-permute-start | bytes 147464 | tf_op jit(solution)/shard_map/ppermute | solution.py:269
  7.1 4.4 %collective-permute-start.1 = (bf16[3,2,32,128]{3,2,1,0:T(8,128)(2,1)S(1)}, bf16[3,2,32,128]{3,2,1,0:T(8,128)(2,1)S(1)}, u32[]{:S(2)}, u32[]{:S(2)}) collective-permute-start(bf16[3,2,32,128]{3,2,1,0:T(8,128)(2,1)S(1)} %get-tuple-element.38), channel_id=1, source_target_pairs={{0,32},{16,48},{32,0},{48,16},{64,96},{80,112},{96,64},{112,80},{1... | collective-permute-start | bytes 147464 | tf_op jit(solution)/shard_map/ppermute | solution.py:269
  7.1 4.5 %collective-permute-start.2 = (bf16[3,2,32,128]{3,2,1,0:T(8,128)(2,1)S(1)}, bf16[3,2,32,128]{3,2,1,0:T(8,128)(2,1)S(1)}, u32[]{:S(2)}, u32[]{:S(2)}) collective-permute-start(bf16[3,2,32,128]{3,2,1,0:T(8,128)(2,1)S(1)} %get-tuple-element.39), channel_id=1, source_target_pairs={{0,48},{16,32},{32,16},{48,0},{64,112},{80,96},{96,80},{112,64},{1... | collective-permute-start | bytes 147464 | tf_op jit(solution)/shard_map/ppermute | solution.py:269
  11.6 5.2 %collective-permute-start.3 = (bf16[3,32,128]{2,1,0:T(8,128)(2,1)S(1)}, bf16[3,32,128]{2,1,0:T(8,128)(2,1)S(1)}, u32[]{:S(2)}, u32[]{:S(2)}) collective-permute-start(bf16[3,32,128]{2,1,0:T(8,128)(2,1)S(1)} %get-tuple-element.40.rest_0_.a_ref), channel_id=1, source_target_pairs={{0,64},{16,80},{32,96},{48,112},{64,0},{80,16},{96,32},{112,48},{1... | collective-permute-start | bytes 73736 | tf_op jit(solution)/shard_map/ppermute | solution.py:269
  13.8 7.8 %collective-permute-start.6 = (bf16[3,32,128]{2,1,0:T(8,128)(2,1)S(1)}, bf16[3,32,128]{2,1,0:T(8,128)(2,1)S(1)}, u32[]{:S(2)}, u32[]{:S(2)}) collective-permute-start(bf16[3,32,128]{2,1,0:T(8,128)(2,1)S(1)} %get-tuple-element.43.a_ref.q4_ref), channel_id=1, source_target_pairs={{0,4},{1,5},{2,6},{3,7},{4,0},{5,1},{6,2},{7,3},{8,12},{9,13},{10,... | collective-permute-start | bytes 73736 | tf_op jit(solution)/shard_map/ppermute | solution.py:269
  16.8 8.6 %collective-permute-start.5 = (bf16[3,64,128]{2,1,0:T(8,128)(2,1)S(1)}, bf16[3,64,128]{2,1,0:T(8,128)(2,1)S(1)}, u32[]{:S(2)}, u32[]{:S(2)}) collective-permute-start(bf16[3,64,128]{2,1,0:T(8,128)(2,1)S(1)} %shard_map.32._.rest_0_.a_ref), channel_id=1, source_target_pairs={{0,192},{16,208},{32,224},{48,240},{64,128},{80,144},{96,160},{112... | collective-permute-start | bytes 147464 | tf_op jit(solution)/shard_map/ppermute | solution.py:269
  20.3 7.2 %collective-permute-start.4 = (bf16[3,128,128]{2,1,0:T(8,128)(2,1)S(1)}, bf16[3,128,128]{2,1,0:T(8,128)(2,1)S(1)}, u32[]{:S(2)}, u32[]{:S(2)}) collective-permute-start(bf16[3,128,128]{2,1,0:T(8,128)(2,1)S(1)} %get-tuple-element.42.rest_0_.a_ref), channel_id=1, source_target_pairs={{0,64},{16,80},{32,96},{48,112},{64,0},{80,16},{96,32},{112,48},{1... | collective-permute-start | bytes 294920 | tf_op jit(solution)/shard_map/ppermute | solution.py:269
  21.6 5.9 %collective-permute-start.7 = (bf16[3,64,128]{2,1,0:T(8,128)(2,1)S(1)}, bf16[3,64,128]{2,1,0:T(8,128)(2,1)S(1)}, u32[]{:S(2)}, u32[]{:S(2)}) collective-permute-start(bf16[3,64,128]{2,1,0:T(8,128)(2,1)S(1)} %shard_map.34.rest_1_.q0_ref), channel_id=1, source_target_pairs={{0,12},{1,13},{2,14},{3,15},{4,8},{5,9},{6,10},{7,11},{8,4},{9,5},... | collective-permute-start | bytes 147464 | tf_op jit(solution)/shard_map/ppermute | solution.py:269
  25.4 3.8 %collective-permute-start.8 = (bf16[3,128,128]{2,1,0:T(8,128)(2,1)S(1)}, bf16[3,128,128]{2,1,0:T(8,128)(2,1)S(1)}, u32[]{:S(2)}, u32[]{:S(2)}) collective-permute-start(bf16[3,128,128]{2,1,0:T(8,128)(2,1)S(1)} %shard_map.36.rest_0_.a_ref), channel_id=1, source_target_pairs={{0,1},{1,0},{2,3},{3,2},{4,5},{5,4},{6,7},{7,6},{8,9},{9,8},{10,11... | collective-permute-start | bytes 294920 | tf_op jit(solution)/shard_map/ppermute | solution.py:269
  29.2 0.9 %copy-start.2 = (f32[2,128,768]{2,1,0:T(8,128)}, f32[2,128,768]{2,1,0:T(8,128)S(1)}, u32[]{:S(2)}) copy-start(f32[2,128,768]{2,1,0:T(8,128)S(1)} %get-tuple-element.54.oe_ref) | copy-start | bytes 2359300
  29.3 13.8 %collective-permute-start.9 = (bf16[2,128,768]{2,1,0:T(8,128)(2,1)S(1)}, bf16[2,128,768]{2,1,0:T(8,128)(2,1)S(1)}, u32[]{:S(2)}, u32[]{:S(2)}) collective-permute-start(bf16[2,128,768]{2,1,0:T(8,128)(2,1)S(1)} %shard_map.40.own_ref), channel_id=1, source_target_pairs={{0,32},{16,48},{32,0},{48,16},{64,96},{80,112},{96,64},{112,80},{1... | collective-permute-start | bytes 1179656 | tf_op jit(solution)/shard_map/ppermute | solution.py:269
  30.1 7.0 %collective-permute-start.11 = (bf16[3,256,128]{2,1,0:T(8,128)(2,1)S(1)}, bf16[3,256,128]{2,1,0:T(8,128)(2,1)S(1)}, u32[]{:S(2)}, u32[]{:S(2)}) collective-permute-start(bf16[3,256,128]{2,1,0:T(8,128)(2,1)S(1)} %shard_map.39.token_ref.kv0_ref.four0_ref), channel_id=1, source_target_pairs={{0,3},{1,2},{2,1},{3,0},{4,7},{5,6},{6,5},{7,4},{8,11},{9,10},{10,... | collective-permute-start | bytes 589832 | tf_op jit(solution)/shard_map/ppermute | solution.py:269
  32.6 8.8 %collective-permute-start.10 = (bf16[3,256,128]{2,1,0:T(8,128)(2,1)S(1)}, bf16[3,256,128]{2,1,0:T(8,128)(2,1)S(1)}, u32[]{:S(2)}, u32[]{:S(2)}) collective-permute-start(bf16[3,256,128]{2,1,0:T(8,128)(2,1)S(1)} %shard_map.37.rest_0_.three0_ref), channel_id=1, source_target_pairs={{0,192},{16,208},{32,224},{48,240},{64,128},{80,144},{96,160},{112... | collective-permute-start | bytes 589832 | tf_op jit(solution)/shard_map/ppermute | solution.py:269
  32.9 20.1 %collective-permute-start.12 = (bf16[2,128,768]{2,1,0:T(8,128)(2,1)S(1)}, bf16[2,128,768]{2,1,0:T(8,128)(2,1)S(1)}, u32[]{:S(2)}, u32[]{:S(2)}) collective-permute-start(bf16[2,128,768]{2,1,0:T(8,128)(2,1)S(1)} %shard_map.40.own_ref), channel_id=1, source_target_pairs={{0,16},{16,0},{32,48},{48,32},{64,80},{80,64},{96,112},{112,96},{1... | collective-permute-start | bytes 1179656 | tf_op jit(solution)/shard_map/ppermute | solution.py:269
  43.1 9.9 %collective-permute-start.13 = (bf16[2,128,768]{2,1,0:T(8,128)(2,1)S(1)}, bf16[2,128,768]{2,1,0:T(8,128)(2,1)S(1)}, u32[]{:S(2)}, u32[]{:S(2)}) collective-permute-start(bf16[2,128,768]{2,1,0:T(8,128)(2,1)S(1)} %shard_map.43.r1_ref), channel_id=1, source_target_pairs={{0,16},{16,0},{32,48},{48,32},{64,80},{80,64},{96,112},{112,96},{1... | collective-permute-start | bytes 1179656 | tf_op jit(solution)/shard_map/ppermute | solution.py:269
  46.6 10.5 %all-to-all-start = ((f32[16,8,128]{2,1,0:T(8,128)}), f32[16,8,128]{2,1,0:T(8,128)S(1)}, u32[]{:S(2)}, u32[]{:S(2)}) async-start(f32[16,8,128]{2,1,0:T(8,128)} %shard_map.41._), calls=%async_computation | async-start | bytes 131072 | tf_op jit(solution)/shard_map/all_to_all | solution.py:337
  50.9 5.5 %collective-permute-start.14 = (f32[3,32,128]{2,1,0:T(8,128)S(1)}, f32[3,32,128]{2,1,0:T(8,128)S(1)}, u32[]{:S(2)}, u32[]{:S(2)}) collective-permute-start(f32[3,32,128]{2,1,0:T(8,128)S(1)} %get-tuple-element.58), channel_id=1, source_target_pairs={{0,16},{16,0},{32,48},{48,32},{64,80},{80,64},{96,112},{112,96},{1... | collective-permute-start | bytes 147464 | tf_op jit(solution)/shard_map/ppermute | solution.py:269
  51.0 5.3 %collective-permute-start.15 = (f32[3,32,128]{2,1,0:T(8,128)S(1)}, f32[3,32,128]{2,1,0:T(8,128)S(1)}, u32[]{:S(2)}, u32[]{:S(2)}) collective-permute-start(f32[3,32,128]{2,1,0:T(8,128)S(1)} %get-tuple-element.59), channel_id=1, source_target_pairs={{0,32},{16,48},{32,0},{48,16},{64,96},{80,112},{96,64},{112,80},{1... | collective-permute-start | bytes 147464 | tf_op jit(solution)/shard_map/ppermute | solution.py:269
  52.7 4.3 %collective-permute-start.16 = (f32[3,32,128]{2,1,0:T(8,128)S(1)}, f32[3,32,128]{2,1,0:T(8,128)S(1)}, u32[]{:S(2)}, u32[]{:S(2)}) collective-permute-start(f32[3,32,128]{2,1,0:T(8,128)S(1)} %get-tuple-element.60), channel_id=1, source_target_pairs={{0,48},{16,32},{32,16},{48,0},{64,112},{80,96},{96,80},{112,64},{1... | collective-permute-start | bytes 147464 | tf_op jit(solution)/shard_map/ppermute | solution.py:269
  53.1 1.1 %copy-start.3 = (f32[2,128,768]{2,1,0:T(8,128)S(1)}, f32[2,128,768]{2,1,0:T(8,128)}, u32[]{:S(2)}) copy-start(f32[2,128,768]{2,1,0:T(8,128)} %copy-done.2) | copy-start | bytes 2359300

commit v2 on v1

--- a/solution.py
+++ b/solution.py
@@ -47,7 +47,7 @@
     )
 
 
-def small_pick_kernel(t_ref, q_ref, kv_ref, own_ref, one_ref, two_ref, three_ref, chunks):
+def small_pick_kernel(q_ref, kv_ref, own_ref, one_ref, two_ref, three_ref, chunks):
     row = lax.broadcasted_iota(jnp.int32, (64, ROWS), 0)
     col = lax.broadcasted_iota(jnp.int32, (64, ROWS), 1)
     j = row & 31
@@ -66,7 +66,7 @@
             t, i = head // 3, head % 3
             chunks[t, i, 0] = jnp.concatenate([k[rs, cs], v[rs, cs]], axis=1).astype(BF)
             chunks[t, i, 1] = jnp.concatenate([q[rs, cs], zeros], axis=1).astype(BF)
-    t = t_ref[0]
+    t = lax.axis_index("gx") & 3
     own_ref[...] = chunks[t]
     one_ref[...] = chunks[t ^ 1]
     two_ref[...] = chunks[t ^ 2]
@@ -114,7 +114,7 @@
                 q2_ref[:, cols] = jnp.where(half[:128], q[:128], q[128:])
 
 
-def level2_kernel(q_ref, own_ref, r1_ref, r2_ref, r3_ref, oe_ref, a_ref, o_ref, e_ref):
+def level2_kernel(q_ref, own_ref, r1_ref, r2_ref, r3_ref, oe_ref, _, a_ref, o_ref, e_ref, unsort_ref):
     half = lanes((128, 128)) < HEAD
     refs = (own_ref, r1_ref, r2_ref, r3_ref)
     for pair in range(HEADS // 2):
@@ -126,17 +126,31 @@
             oe_ref[0, :, cols], oe_ref[1, :, cols],
             jnp.where(half, out[:n], out[n:]), jnp.where(half, log[:n], log[n:]),
         )
-        a_ref[:, cols] = o.astype(BF)
+        second = o.astype(BF)
+        for side in range(2):
+            start = (2 * pair + side) % 4 * 128
+            rows = slice(start, start + 128)
+            one, other = (second, a_ref[rows, cols]) if side == 0 else (a_ref[rows, cols], second)
+            a_ref[rows, cols] = jnp.where(half, one, other)
         low = pair // 2 * 32
         o_ref[:, cols] = o[low : low + 32]
         e_ref[:, cols] = e[low : low + 32]
-
-
-def regroup4_kernel(own_ref, r1_ref, r2_ref, r3_ref, kv4_ref, q4_ref):
+    row = lax.broadcasted_iota(jnp.int32, (ROWS, ROWS), 0)
+    col = lax.broadcasted_iota(jnp.int32, (ROWS, ROWS), 1)
+    unsort_ref[...] = (row == sorted_position(col)).astype(F32).astype(BF)
+
+
+def regroup4_kernel(own_ref, r1_ref, r2_ref, r3_ref, kv4_ref, q4_ref, q5_ref):
     refs = (own_ref, r1_ref, r2_ref, r3_ref)
+    fifth = [[], [], [], []]
     for i in range(3):
         kv4_ref[i] = jnp.concatenate([r[i, 0].astype(F32)[:8] for r in refs], axis=0).astype(BF)
-        q4_ref[i] = jnp.concatenate([r[i, 1].astype(F32)[:8] for r in refs], axis=0).astype(BF)
+        q = [r[i, 1].astype(F32)[:8] for r in refs]
+        q4_ref[i] = jnp.concatenate(q, axis=0).astype(BF)
+        for n in range(4):
+            fifth[n].append(q[n][:2])
+    empty = jnp.zeros((2, 128), F32)
+    q5_ref[...] = jnp.concatenate([x for rows in fifth for x in rows + [empty]], axis=0).astype(BF)
 
 
 def regroup3_kernel(own_ref, r1_ref, r2_ref, r3_ref, _, kv_ref, q_ref):
@@ -148,10 +162,9 @@
 
 def join_kernel(a_ref, b_ref, *rest):
     out_ref = rest[-1]
-    n = a_ref.shape[1]
-    for i in range(3):
-        out_ref[i, :n] = a_ref[i]
-        out_ref[i, n:] = b_ref[i]
+    n = a_ref.shape[-2]
+    out_ref[..., :n, :] = a_ref[...]
+    out_ref[..., n:, :] = b_ref[...]
 
 
 def gate_kernel(a_ref, token_ref, out_ref):
@@ -165,21 +178,21 @@
     return (w1 * o1 + w2 * o2) / den, top + jnp.log(den) * LOG2E
 
 
-def level5_kernel(t_ref, q0_ref, q1_ref, kv0_ref, kv1_ref, fifth_ref):
-    t, y = t_ref[0], t_ref[1]
+def level5_kernel(q0_ref, q1_ref, kv0_ref, kv1_ref, fifth_ref):
+    t, y = lax.axis_index("gx") & 3, lax.axis_index("gy") >> 2
     half = lanes((128, 128)) < HEAD
+    row_head = (lax.broadcasted_iota(jnp.int32, (128, 128), 0) & 7) >> 1
     in_five = (lanes((128, 512)) & 7) < 2
-    fifth_ref[...] = jnp.zeros_like(fifth_ref)
+    q = jnp.concatenate([q0_ref[...], q1_ref[...]], axis=0)
+    both = jnp.zeros((128, 128), F32)
     for i in range(3):
         kv = jnp.concatenate([kv0_ref[i], kv1_ref[i]], axis=0)
-        q = jnp.concatenate([q0_ref[i], q1_ref[i]], axis=0)
-        p, inv, log5 = softmax_parts(jnp.where(in_five, dot_t(q, kv), LOW))
-        out5 = dot(p, kv) * inv
-        both = jnp.where(half, log5, out5)
-        for m, apart in enumerate((0, 1, 3, 2)):
-            for n in range(4):
-                slot = (t ^ n) * 4 + (y ^ apart)
-                fifth_ref[slot, 2 * i : 2 * i + 2, :] = both[m * 32 + n * 8 : m * 32 + n * 8 + 2]
+        p, inv, log = softmax_parts(jnp.where(in_five, dot_t(q, kv), LOW))
+        both = jnp.where(row_head == i, jnp.where(half, log, dot(p, kv) * inv), both)
+    for m in range(4):
+        for n in range(4):
+            row = m * 32 + n * 8
+            fifth_ref[(t ^ n) * 4 + (y ^ m)] = both[row : row + 8]
 
 
 def level34_kernel(q_ref, three0_ref, three1_ref, q4_ref, four0_ref, four1_ref, _, *outs):
@@ -200,51 +213,47 @@
 
 
 def final_kernel(
-    t_ref, a_ref, second_ref, o_ref, e_ref, own_ref, one_ref, two_ref, three_ref, fifth_ref,
-    out_ref, rows_ref, back,
+    a_ref, o_ref, e_ref, unsort_ref, own_ref, one_ref, two_ref, three_ref, fifth_ref,
+    out_ref, rows_ref, back, fives,
 ):
-    t = t_ref[0]
+    t = lax.axis_index("gx") & 3
     for n, r in enumerate((own_ref, one_ref, two_ref, three_ref)):
         back[n] = r[...]
-    half = lanes((128, 128)) < HEAD
+    half8 = lanes((8, 128)) < HEAD
+    half = lanes((32, 128)) < HEAD
+    for source in range(4):
+        pieces = [fifth_ref[source * 4 + m] for m in range(4)]
+        logs = [x[:, :1] for x in pieces]
+        top = functools.reduce(jnp.maximum, logs)
+        w = [jnp.exp2(x - top) for x in logs]
+        den = sum(w)
+        num = sum(wi * x for wi, x in zip(w, pieces))
+        fives[source] = jnp.where(half8, top + jnp.log(den) * LOG2E, num / den)
     rows_ref[...] = a_ref[...]
     for pair in range(HEADS // 2):
         cols = slice(pair * 128, pair * 128 + 128)
-        second = second_ref[:, cols]
+        got = []
+        for head in (2 * pair, 2 * pair + 1):
+            source, i = head // 3, head % 3
+            x = back[t ^ source, i]
+            five = fives[source, 2 * i : 2 * i + 2, :]
+            o, e = mix(x[:2], x[:2, :1], five, five[:, :1])
+            got.append(jnp.concatenate([jnp.where(half8[:2], e, o), x[2:]], axis=0))
+        e = jnp.concatenate([got[0][:, :HEAD], got[1][:, :HEAD]], axis=1)
+        o = jnp.concatenate([got[0][:, HEAD:], got[1][:, HEAD:]], axis=1)
+        mixed = mix(o_ref[:, cols], e_ref[:, cols], o, e)[0].astype(BF)
         for side in range(2):
-            mine = half if side == 0 else jnp.logical_not(half)
-            start = (2 * pair + side) % 4 * 128
-            rows = slice(start, start + 128)
-            rows_ref[rows, cols] = jnp.where(mine, second, rows_ref[rows, cols])
-    for head in range(HEADS):
-        source, i = head // 3, head % 3
-        got = back[t ^ source, i]
-        pieces = [fifth_ref[source * 4 + m, 2 * i : 2 * i + 2, :] for m in range(4)]
-        e, o = got[:, :HEAD], got[:, HEAD:]
-        e2, o2 = e[:2], o[:2]
-        logs = [x[:, :HEAD] for x in pieces]
-        top = functools.reduce(jnp.maximum, logs, e2)
-        w = [jnp.exp2(x - top) for x in logs]
-        w2 = jnp.exp2(e2 - top)
-        den = sum(w, w2)
-        num = sum((wi * x[:, HEAD:] for wi, x in zip(w, pieces)), w2 * o2)
-        o = jnp.concatenate([num / den, o[2:]], axis=0)
-        e = jnp.concatenate([top + jnp.log(den) * LOG2E, e[2:]], axis=0)
-        cols = slice(head * HEAD, head * HEAD + HEAD)
-        mixed, _ = mix(o_ref[:, cols], e_ref[:, cols], o, e)
-        base = head % 4 * 128 + head // 4 * 32
-        rows_ref[base : base + 32, cols] = mixed.astype(BF)
-    row = lax.broadcasted_iota(jnp.int32, (ROWS, ROWS), 0)
-    col = lax.broadcasted_iota(jnp.int32, (ROWS, ROWS), 1)
-    onehot = (row == sorted_position(col)).astype(F32).astype(BF)
-    for pair in range(HEADS // 2):
-        cols = pl.ds(pair * 128, 128)
-        out_ref[0, :, cols] = dot(onehot, rows_ref[:, cols]).astype(BF)
+            start = (2 * pair + side) % 4 * 128 + pair // 2 * 32
+            rows = slice(start, start + 32)
+            one, other = (mixed, rows_ref[rows, cols]) if side == 0 else (rows_ref[rows, cols], mixed)
+            rows_ref[rows, cols] = jnp.where(half, one, other)
+        if pair % 2:
+            wide = slice(pair * 128 - 128, pair * 128 + 128)
+            out_ref[0, :, wide] = dot(unsort_ref[...], rows_ref[:, wide]).astype(BF)
 
 
 VMEM = pl.BlockSpec(memory_space=pltpu.VMEM)
 ANY = pl.BlockSpec(memory_space=pl.ANY)
-SMEM = pl.BlockSpec(memory_space=pltpu.SMEM)
 
 
 def call(kernel, outs, in_specs=None, scratch=(), flops=0, nbytes=0, limit=24, **more):
@@ -270,30 +279,27 @@
 
 
 def per_device(queries, key_values):
-    gx, gy = lax.axis_index("gx"), lax.axis_index("gy")
-    place = jnp.stack([gx & 3, gy >> 2]).astype(jnp.int32)
-
     chunk = ((3, 2, 32, 128), BF)
     own, c1, c2, c3 = call(
-        small_pick_kernel, [chunk] * 4, [SMEM, VMEM, VMEM], [pltpu.VMEM((4, 3, 2, 32, 128), BF)],
+        small_pick_kernel, [chunk] * 4, [VMEM, VMEM], [pltpu.VMEM((4, 3, 2, 32, 128), BF)],
         nbytes=3 << 20,
-    )(place, queries, key_values)
+    )(queries, key_values)
     g = [own] + [permute(c, "gx", lambda i, n=n: i ^ n) for n, c in ((1, c1), (2, c2), (3, c3))]
 
     qs, ks, vs, send2 = call(
         sort_kernel, [((ROWS, WIDTH), BF)] * 3 + [((2, 128, WIDTH), BF)], nbytes=6 << 20
     )(queries, key_values)
 
-    def level1(n, *tokens, held=()):
+    def level1(n, *tokens, held=(), cost=1 << 31):
         return call(
             functools.partial(level1_kernel, 2 * n),
             [((ROWS, WIDTH), BF), ((2, 128, WIDTH), F32), ((128, WIDTH), BF)],
-            [VMEM] * 3 + [ANY] * len(tokens) + [VMEM] * len(held), flops=1 << 31, nbytes=2 << 20,
+            [VMEM] * 3 + [ANY] * len(tokens) + [VMEM] * len(held), flops=cost, nbytes=1 << 18,
             input_output_aliases={3 + len(tokens) + i: i for i in range(len(held))},
         )(qs, ks, vs, *tokens, *held)
 
     def join(a, b, *tokens):
-        shape = (a.shape[0], 2 * a.shape[1], a.shape[2])
+        shape = a.shape[:-2] + (2 * a.shape[-2], a.shape[-1])
         return call(join_kernel, [(shape, BF)], [VMEM] * 2 + [ANY] * len(tokens), nbytes=1 << 18, limit=4)(
             a, b, *tokens
         )[0]
@@ -303,9 +309,9 @@
             gate_kernel, [(x.shape, x.dtype)], [ANY, ANY], out_specs=[ANY], input_output_aliases={0: 0}, limit=4
         )(x, token)[0]
 
-    kv4, q4 = call(regroup4_kernel, [((3, 32, 128), BF)] * 2, nbytes=1 << 19, limit=4)(*g)
+    kv4, q4, q5 = call(regroup4_kernel, [((3, 32, 128), BF)] * 2 + [((32, 128), BF)], nbytes=1 << 19, limit=4)(*g)
     z4 = permute(kv4, "gx", lambda i: i ^ 4)
-    y5 = permute(q4, "gy", lambda i: i ^ 4)
+    y5 = permute(q5, "gy", lambda i: i ^ 4)
     held = level1(0, kv4)
     kv4 = join(kv4, z4, held[2])
     z4 = permute(kv4, "gx", lambda i: i ^ 12)
@@ -313,21 +319,22 @@
         *g, kv4
     )
     z3 = permute(kv3, "gx", lambda i: i ^ 4)
-    q5 = join(q4, y5, kv4)
-    y5 = permute(q5, "gy", lambda i: i ^ 12)
+    q5 = join(q5, y5, kv4)
     held = level1(1, kv3, q5, held=held)
     kv4 = join(kv4, z4, held[2])
     x4 = permute(kv4, "gy", lambda i: i ^ 1)
-    kv3 = join(kv3, z3, kv4)
-    z3 = permute(kv3, "gx", lambda i: i ^ 12)
-    held = level1(2, kv3, y5, held=held)
-    kv4 = join(kv4, x4, held[2])
-    x4 = permute(kv4, "gy", lambda i: i ^ 3)
     send2 = gate(send2, kv4)
     far2 = permute(send2, "gx", lambda i: i ^ 2)
     near2 = permute(send2, "gx", lambda i: i ^ 1)
-    (fifth,) = call(level5_kernel, [((16, 8, 128), F32)], [SMEM] + [VMEM] * 4, nbytes=1 << 20)(
-        place, q5, y5, kv4, x4
+    kv3 = join(kv3, z3, kv4)
+    z3 = permute(kv3, "gx", lambda i: i ^ 12)
+    held = level1(2, kv3, send2, held=held)
+    kv4 = join(kv4, x4, held[2])
+    x4 = permute(kv4, "gy", lambda i: i ^ 2)
+    q5 = gate(q5, kv4)
+    y5 = permute(q5, "gy", lambda i: i ^ 8)
+    (fifth,) = call(level5_kernel, [((16, 8, 128), F32)], [VMEM] * 4, nbytes=1 << 20)(
+        q5, y5, kv4, x4
     )
     groups = [
         [(4 * zg + t) * 16 + (4 * y + x) for t in range(4) for y in range(4)]
@@ -341,15 +348,17 @@
     )
     far2 = gate(far2, p0)
     other2 = permute(far2, "gx", lambda i: i ^ 1)
-    second, o12, e12 = call(
-        level2_kernel, [((128, WIDTH), BF), ((32, WIDTH), F32), ((32, WIDTH), F32)],
-        flops=1 << 31, nbytes=3 << 20,
-    )(held[2], send2, far2, near2, other2, held[1])
+    attended, o12, e12, unsort = call(
+        level2_kernel,
+        [((ROWS, WIDTH), BF), ((32, WIDTH), F32), ((32, WIDTH), F32), ((ROWS, ROWS), BF)],
+        flops=1 << 31, nbytes=3 << 20, input_output_aliases={6: 0},
+    )(held[2], send2, far2, near2, other2, held[1], held[0])
     back = [p0] + [permute(x, "gx", lambda i, n=n: i ^ n) for n, x in ((1, p1), (2, p2), (3, p3))]
     (out,) = call(
-        final_kernel, [((1, ROWS, WIDTH), BF)], [SMEM] + [VMEM] * 9,
-        [pltpu.VMEM((ROWS, WIDTH), BF), pltpu.VMEM((4, 3, 32, 128), F32)], nbytes=4 << 20,
-    )(place, held[0], second, o12, e12, *back, spread)
+        final_kernel, [((1, ROWS, WIDTH), BF)], [VMEM] * 9,
+        [pltpu.VMEM((ROWS, WIDTH), BF), pltpu.VMEM((4, 3, 32, 128), F32), pltpu.VMEM((4, 8, 128), F32)],
+        nbytes=4 << 20,
+    )(attended, o12, e12, unsort, *back, spread)
     return out
 
 

time: 60.1 us -> 58.7 us (0.977)
  waiting for transfers between devices: 3.65 us -> 2.41 us
  Pallas kernels: 17.6 us -> 16.4 us
  local copies, waits for them, and re-layouts: 3.76 us -> 4.55 us
    all_to_all x1, starting transfers between devices: 4.27 us -> 5.88 us  [per_device(): spread = lax.all_to_all(fifth, ('gx', 'gy'), 0, 0, axis_index_groups=groups)]
    ppermute x17, starting transfers between devices: 30.3 us -> 29 us  [permute(): lax.ppermute(x, axis, [(i, partner(i)) for i in range(lax.axis_size(axis))])]
    ppermute x17, waiting for transfers between devices: 3.64 us -> 2.4 us  [permute(): lax.ppermute(x, axis, [(i, partner(i)) for i in range(lax.axis_size(axis))])]
    pallas_call x18 -> x19, Pallas kernels: 17.6 us -> 16.4 us  [run(): pl.pallas_call(kernel, out_shape=[jax.ShapeDtypeStruct(s, d) for s, d in...]
    unnamed x8, local copies, waits for them, and re-layouts: 3.76 us -> 4.55 us
  transfers between devices with their start and end apart: 18 -> 18, of which waited for: 4 -> 3; matrix products, arithmetic and copies ran while one was open for 0% -> 0% of each run, Pallas kernels for 23% -> 24%
where the time goes in v2:
time: 58.7 us; the launch traced here: 58.4 us
  starting transfers between devices  34.9 us (59%)
  Pallas kernels  16.4 us (28%)
  local copies, waits for them, and re-layouts  4.55 us (8%)
  waiting for transfers between devices  2.41 us (4%)
    ppermute x17, starting transfers between devices, permute(): lax.ppermute(x, axis, [(i, partner(i)) for i in range(lax.axis_size(axis))])  29 us
    pallas_call x19, Pallas kernels, run(): pl.pallas_call(kernel, out_shape=[jax.ShapeDtypeStruct(s, d) for s, d in...  16.4 us
    all_to_all x1, starting transfers between devices, per_device(): spread = lax.all_to_all(fifth, ('gx', 'gy'), 0, 0, axis_index_groups=groups)  5.88 us
    unnamed x8, local copies, waits for them, and re-layouts  4.55 us
    ppermute x17, waiting for transfers between devices, permute(): lax.ppermute(x, axis, [(i, partner(i)) for i in range(lax.axis_size(axis))])  2.4 us
  transfers between devices with their start and end apart: 18, of which 3 were waited for; matrix products, arithmetic and copies ran while one was open for 0% of the time, Pallas kernels for 24%

profile of v2, /device:TPU:1, one launch (start us, length us, event | category | flops | bytes accessed | tf_op | source)
XLA Modules:
  0.0 58.4 jit_solution(14097550705830330765)
XLA Ops:
  0.0 1.4 %copy-done = bf16[2,1,512,768]{3,2,1,0:T(8,128)(2,1)S(1)} copy-done((bf16[2,1,512,768]{3,2,1,0:T(8,128)(2,1)S(1)}, bf16[2,1,512,768]{3,2,1,0:T(8,128)(2,1)}, u32[]{:S(2)}) %copy-start) | copy-done | bytes 1572888
  1.4 1.1 %copy-done.1 = bf16[1,512,768]{2,1,0:T(8,128)(2,1)S(1)} copy-done((bf16[1,512,768]{2,1,0:T(8,128)(2,1)S(1)}, bf16[1,512,768]{2,1,0:T(8,128)(2,1)}, u32[]{:S(2)}) %copy-start.1) | copy-done | bytes 786456
  3.1 3.3 %collective-permute-start = (bf16[3,2,32,128]{3,2,1,0:T(8,128)(2,1)S(1)}, bf16[3,2,32,128]{3,2,1,0:T(8,128)(2,1)S(1)}, u32[]{:S(2)}, u32[]{:S(2)}) collective-permute-start(bf16[3,2,32,128]{3,2,1,0:T(8,128)(2,1)S(1)} %get-tuple-element.39), channel_id=1, source_target_pairs={{0,16},{16,0},{32,48},{48,32},{64,80},{80,64},{96,112},{112,96},{1... | collective-permute-start | bytes 147464 | tf_op jit(solution)/shard_map/ppermute | solution.py:278
  6.4 1.7 %collective-permute-start.2 = (bf16[3,2,32,128]{3,2,1,0:T(8,128)(2,1)S(1)}, bf16[3,2,32,128]{3,2,1,0:T(8,128)(2,1)S(1)}, u32[]{:S(2)}, u32[]{:S(2)}) collective-permute-start(bf16[3,2,32,128]{3,2,1,0:T(8,128)(2,1)S(1)} %get-tuple-element.41), channel_id=1, source_target_pairs={{0,48},{16,32},{32,16},{48,0},{64,112},{80,96},{96,80},{112,64},{1... | collective-permute-start | bytes 147464 | tf_op jit(solution)/shard_map/ppermute | solution.py:278
  8.2 2.7 %shard_map.28 = (bf16[512,768]{1,0:T(8,128)(2,1)S(1)}, bf16[512,768]{1,0:T(8,128)(2,1)S(1)}, bf16[512,768]{1,0:T(8,128)(2,1)S(1)}, bf16[2,128,768]{2,1,0:T(8,128)(2,1)S(1)}) custom-call(bf16[1,512,768]{2,1,0:T(8,128)(2,1)S(1)} %copy-done.1, bf16[2,1,512,768]{3,2,1,0:T(8,128)(2,1)S(1)} %copy-done), custom_call_target="tpu_custom_call" | custom-call | bytes 6291456 | tf_op jit(solution)/shard_map/pallas_call | solution.py:263
  11.0 2.2 %collective-permute-start.3 = (bf16[3,32,128]{2,1,0:T(8,128)(2,1)S(1)}, bf16[3,32,128]{2,1,0:T(8,128)(2,1)S(1)}, u32[]{:S(2)}, u32[]{:S(2)}) collective-permute-start(bf16[3,32,128]{2,1,0:T(8,128)(2,1)S(1)} %get-tuple-element.42.rest_0_.a_ref), channel_id=1, source_target_pairs={{0,64},{16,80},{32,96},{48,112},{64,0},{80,16},{96,32},{112,48},{1... | collective-permute-start | bytes 73736 | tf_op jit(solution)/shard_map/ppermute | solution.py:278
  13.2 1.3 %collective-permute-start.6 = (bf16[32,128]{1,0:T(8,128)(2,1)S(1)}, bf16[32,128]{1,0:T(8,128)(2,1)S(1)}, u32[]{:S(2)}, u32[]{:S(2)}) collective-permute-start(bf16[32,128]{1,0:T(8,128)(2,1)S(1)} %get-tuple-element.45.a_ref), channel_id=1, source_target_pairs={{0,4},{1,5},{2,6},{3,7},{4,0},{5,1},{6,2},{7,3},{8,12},{9,13},{10,... | collective-permute-start | bytes 24584 | tf_op jit(solution)/shard_map/ppermute | solution.py:278
  14.5 1.7 %shard_map.31 = (bf16[512,768]{1,0:T(8,128)(2,1)S(1)}, f32[2,128,768]{2,1,0:T(8,128)S(1)}, bf16[128,768]{1,0:T(8,128)(2,1)S(1)}) custom-call(bf16[512,768]{1,0:T(8,128)(2,1)S(1)} %get-tuple-element.35.q_ref, bf16[512,768]{1,0:T(8,128)(2,1)S(1)} %get-tuple-element.36.k_ref, bf16[512,768]{1,0:T(8,128)(2,1)S(1)} %get-tuple-element.37.v_ref, ...), custom_call_target="tpu_custom_call" | custom-call | flops 2147483648 | bytes 262144 | tf_op jit(solution)/shard_map/pallas_call | solution.py:263
  16.2 3.5 %collective-permute-start.5 = (bf16[3,64,128]{2,1,0:T(8,128)(2,1)S(1)}, bf16[3,64,128]{2,1,0:T(8,128)(2,1)S(1)}, u32[]{:S(2)}, u32[]{:S(2)}) collective-permute-start(bf16[3,64,128]{2,1,0:T(8,128)(2,1)S(1)} %shard_map.32._.rest_0_.a_ref), channel_id=1, source_target_pairs={{0,192},{16,208},{32,224},{48,240},{64,128},{80,144},{96,160},{112... | collective-permute-start | bytes 147464 | tf_op jit(solution)/shard_map/ppermute | solution.py:278
  19.7 1.3 %collective-permute-start.4 = (bf16[3,128,128]{2,1,0:T(8,128)(2,1)S(1)}, bf16[3,128,128]{2,1,0:T(8,128)(2,1)S(1)}, u32[]{:S(2)}, u32[]{:S(2)}) collective-permute-start(bf16[3,128,128]{2,1,0:T(8,128)(2,1)S(1)} %get-tuple-element.44.rest_0_.a_ref), channel_id=1, source_target_pairs={{0,64},{16,80},{32,96},{48,112},{64,0},{80,16},{96,32},{112,48},{1... | collective-permute-start | bytes 294920 | tf_op jit(solution)/shard_map/ppermute | solution.py:278
  21.0 1.7 %shard_map.35 = (bf16[512,768]{1,0:T(8,128)(2,1)S(1)}, f32[2,128,768]{2,1,0:T(8,128)S(1)}, bf16[128,768]{1,0:T(8,128)(2,1)S(1)}) custom-call(bf16[512,768]{1,0:T(8,128)(2,1)S(1)} %get-tuple-element.35.q_ref, bf16[512,768]{1,0:T(8,128)(2,1)S(1)} %get-tuple-element.36.k_ref, ...), custom_call_target="tpu_custom_call", output_to_operand_aliasing={{0}: (5, {}), {1}: (6, {}), {2}: (7, {})} | custom-call | flops 2147483648 | bytes 262144 | tf_op jit(solution)/shard_map/pallas_call | solution.py:263
  22.7 1.3 %collective-permute-start.9 = (bf16[3,128,128]{2,1,0:T(8,128)(2,1)S(1)}, bf16[3,128,128]{2,1,0:T(8,128)(2,1)S(1)}, u32[]{:S(2)}, u32[]{:S(2)}) collective-permute-start(bf16[3,128,128]{2,1,0:T(8,128)(2,1)S(1)} %shard_map.36.rest_0_.token_ref.a_ref), channel_id=1, source_target_pairs={{0,1},{1,0},{2,3},{3,2},{4,5},{5,4},{6,7},{7,6},{8,9},{9,8},{10,11... | collective-permute-start | bytes 294920 | tf_op jit(solution)/shard_map/ppermute | solution.py:278
  24.7 2.2 %collective-permute-done.4.b_ref = bf16[3,128,128]{2,1,0:T(8,128)(2,1)S(1)} collective-permute-done((bf16[3,128,128]{2,1,0:T(8,128)(2,1)S(1)}, bf16[3,128,128]{2,1,0:T(8,128)(2,1)S(1)}, u32[]{:S(2)}, u32[]{:S(2)}) %collective-permute-start.4) | collective-permute-done | bytes 98336 | tf_op jit(solution)/shard_map/ppermute | solution.py:278
  26.9 1.7 %shard_map.39 = (bf16[512,768]{1,0:T(8,128)(2,1)S(1)}, f32[2,128,768]{2,1,0:T(8,128)S(1)}, bf16[128,768]{1,0:T(8,128)(2,1)S(1)}) custom-call(bf16[512,768]{1,0:T(8,128)(2,1)S(1)} %get-tuple-element.35.q_ref, bf16[512,768]{1,0:T(8,128)(2,1)S(1)} %get-tuple-element.36.k_ref, ...), custom_call_target="tpu_custom_call", output_to_operand_aliasing={{0}: (5, {}), {1}: (6, {}), {2}: (7, {})} | custom-call | flops 2147483648 | bytes 262144 | tf_op jit(solution)/shard_map/pallas_call | solution.py:263
  29.5 2.8 %collective-permute-start.10 = (bf16[3,256,128]{2,1,0:T(8,128)(2,1)S(1)}, bf16[3,256,128]{2,1,0:T(8,128)(2,1)S(1)}, u32[]{:S(2)}, u32[]{:S(2)}) collective-permute-start(bf16[3,256,128]{2,1,0:T(8,128)(2,1)S(1)} %shard_map.40.token_ref.kv0_ref.four0_ref), channel_id=1, source_target_pairs={{0,2},{1,3},{2,0},{3,1},{4,6},{5,7},{6,4},{7,5},{8,10},{9,11},{10,... | collective-permute-start | bytes 589832 | tf_op jit(solution)/shard_map/ppermute | solution.py:278
  32.4 2.3 %collective-permute-start.11 = (bf16[64,128]{1,0:T(8,128)(2,1)S(1)}, bf16[64,128]{1,0:T(8,128)(2,1)S(1)}, u32[]{:S(2)}, u32[]{:S(2)}) collective-permute-start(bf16[64,128]{1,0:T(8,128)(2,1)S(1)} %shard_map.41.q0_ref), channel_id=1, source_target_pairs={{0,8},{1,9},{2,10},{3,11},{4,12},{5,13},{6,14},{7,15},{8,0},{9,1},... | collective-permute-start | bytes 49160 | tf_op jit(solution)/shard_map/ppermute | solution.py:278
  34.6 4.3 %collective-permute-start.12 = (bf16[2,128,768]{2,1,0:T(8,128)(2,1)S(1)}, bf16[2,128,768]{2,1,0:T(8,128)(2,1)S(1)}, u32[]{:S(2)}, u32[]{:S(2)}) collective-permute-start(bf16[2,128,768]{2,1,0:T(8,128)(2,1)S(1)} %shard_map.38.rest_1_.own_ref), channel_id=1, source_target_pairs={{0,16},{16,0},{32,48},{48,32},{64,80},{80,64},{96,112},{112,96},{1... | collective-permute-start | bytes 1179656 | tf_op jit(solution)/shard_map/ppermute | solution.py:278
  39.0 1.6 %shard_map.42._ = f32[16,8,128]{2,1,0:T(8,128)} custom-call(bf16[64,128]{1,0:T(8,128)(2,1)S(1)} %shard_map.41.q0_ref, bf16[64,128]{1,0:T(8,128)(2,1)S(1)} %collective-permute-done.11.q1_ref, bf16[3,256,128]{2,1,0:T(8,128)(2,1)S(1)} %shard_map.40.token_ref.kv0_ref.four0_ref, bf16[3,256,128]{2,1,0:T(8,128)(2,1)S(1)} %collective-permute-done.10.kv1_ref.four1_ref), custom_call_target="tpu_custom_call" | custom-call | bytes 1048576 | tf_op jit(solution)/shard_map/pallas_call | solution.py:263
  40.5 2.3 %shard_map.43 = (f32[3,32,128]{2,1,0:T(8,128)S(1)}, f32[3,32,128]{2,1,0:T(8,128)}, f32[3,32,128]{2,1,0:T(8,128)}, f32[3,32,128]{2,1,0:T(8,128)}) custom-call(bf16[3,128,128]{2,1,0:T(8,128)(2,1)S(1)} %get-tuple-element.53.q_ref, bf16[3,256,128]{2,1,0:T(8,128)(2,1)S(1)} %shard_map.37.rest_0_.three0_ref, ...), custom_call_target="tpu_custom_call" | custom-call | bytes 1048576 | tf_op jit(solution)/shard_map/pallas_call | solution.py:263
  42.9 2.0 %collective-permute-start.13 = (bf16[2,128,768]{2,1,0:T(8,128)(2,1)S(1)}, bf16[2,128,768]{2,1,0:T(8,128)(2,1)S(1)}, u32[]{:S(2)}, u32[]{:S(2)}) collective-permute-start(bf16[2,128,768]{2,1,0:T(8,128)(2,1)S(1)} %shard_map.44.r1_ref), channel_id=1, source_target_pairs={{0,16},{16,0},{32,48},{48,32},{64,80},{80,64},{96,112},{112,96},{1... | collective-permute-start | bytes 1179656 | tf_op jit(solution)/shard_map/ppermute | solution.py:278
  44.9 5.9 %all-to-all-start = ((f32[16,8,128]{2,1,0:T(8,128)}), f32[16,8,128]{2,1,0:T(8,128)S(1)}, u32[]{:S(2)}, u32[]{:S(2)}) async-start(f32[16,8,128]{2,1,0:T(8,128)} %shard_map.42._), calls=%async_computation | async-start | bytes 131072 | tf_op jit(solution)/shard_map/all_to_all | solution.py:344
  51.0 1.6 %collective-permute-start.15 = (f32[3,32,128]{2,1,0:T(8,128)}, f32[3,32,128]{2,1,0:T(8,128)S(1)}, u32[]{:S(2)}, u32[]{:S(2)}) collective-permute-start(f32[3,32,128]{2,1,0:T(8,128)} %get-tuple-element.63), channel_id=1, source_target_pairs={{0,32},{16,48},{32,0},{48,16},{64,96},{80,112},{96,64},{112,80},{1... | collective-permute-start | bytes 147464 | tf_op jit(solution)/shard_map/ppermute | solution.py:278
  54.1 2.4 %shard_map.45 = (bf16[512,768]{1,0:T(8,128)(2,1)S(1)}, f32[32,768]{1,0:T(8,128)S(1)}, f32[32,768]{1,0:T(8,128)S(1)}, bf16[512,512]{1,0:T(8,128)(2,1)S(1)}) custom-call(bf16[128,768]{1,0:T(8,128)(2,1)S(1)} %get-tuple-element.52.rest_0_.q_ref, bf16[2,128,768]{2,1,0:T(8,128)(2,1)S(1)} %shard_map.38.rest_1_.own_ref, ...), custom_call_target="tpu_custom_call", output_to_operand_aliasing={{0}: (6, {})} | custom-call | flops 2147483648 | bytes 3145728 | tf_op jit(solution)/shard_map/pallas_call | solution.py:263
  56.6 1.8 %shard_map.46 = bf16[1,512,768]{2,1,0:T(8,128)(2,1)} custom-call(bf16[512,768]{1,0:T(8,128)(2,1)S(1)} %get-tuple-element.58.a_ref, f32[32,768]{1,0:T(8,128)S(1)} %get-tuple-element.59.o_ref, f32[32,768]{1,0:T(8,128)S(1)} %get-tuple-element.60.e_ref, bf16[512,512]{1,0:T(8,128)(2,1)S(1)} %get-tuple-element.61.unsort_ref, ...), custom_call_target="tpu_custom_call" | custom-call | bytes 4194304 | tf_op jit(solution)/shard_map/pallas_call | solution.py:263
  (39 shorter events, 4.2 us)
Async XLA Ops:
  0.0 1.4 %copy-start = (bf16[2,1,512,768]{3,2,1,0:T(8,128)(2,1)S(1)}, bf16[2,1,512,768]{3,2,1,0:T(8,128)(2,1)}, u32[]{:S(2)}) copy-start(bf16[2,1,512,768]{3,2,1,0:T(8,128)(2,1)} %kv_ref.3) | copy-start | bytes 4718596
  1.4 1.1 %copy-start.1 = (bf16[1,512,768]{2,1,0:T(8,128)(2,1)S(1)}, bf16[1,512,768]{2,1,0:T(8,128)(2,1)}, u32[]{:S(2)}) copy-start(bf16[1,512,768]{2,1,0:T(8,128)(2,1)} %q_ref.3) | copy-start | bytes 2359300
  3.1 7.7 %collective-permute-start = (bf16[3,2,32,128]{3,2,1,0:T(8,128)(2,1)S(1)}, bf16[3,2,32,128]{3,2,1,0:T(8,128)(2,1)S(1)}, u32[]{:S(2)}, u32[]{:S(2)}) collective-permute-start(bf16[3,2,32,128]{3,2,1,0:T(8,128)(2,1)S(1)} %get-tuple-element.39), channel_id=1, source_target_pairs={{0,16},{16,0},{32,48},{48,32},{64,80},{80,64},{96,112},{112,96},{1... | collective-permute-start | bytes 147464 | tf_op jit(solution)/shard_map/ppermute | solution.py:278
  6.4 4.4 %collective-permute-start.1 = (bf16[3,2,32,128]{3,2,1,0:T(8,128)(2,1)S(1)}, bf16[3,2,32,128]{3,2,1,0:T(8,128)(2,1)S(1)}, u32[]{:S(2)}, u32[]{:S(2)}) collective-permute-start(bf16[3,2,32,128]{3,2,1,0:T(8,128)(2,1)S(1)} %get-tuple-element.40), channel_id=1, source_target_pairs={{0,32},{16,48},{32,0},{48,16},{64,96},{80,112},{96,64},{112,80},{1... | collective-permute-start | bytes 147464 | tf_op jit(solution)/shard_map/ppermute | solution.py:278
  6.4 4.5 %collective-permute-start.2 = (bf16[3,2,32,128]{3,2,1,0:T(8,128)(2,1)S(1)}, bf16[3,2,32,128]{3,2,1,0:T(8,128)(2,1)S(1)}, u32[]{:S(2)}, u32[]{:S(2)}) collective-permute-start(bf16[3,2,32,128]{3,2,1,0:T(8,128)(2,1)S(1)} %get-tuple-element.41), channel_id=1, source_target_pairs={{0,48},{16,32},{32,16},{48,0},{64,112},{80,96},{96,80},{112,64},{1... | collective-permute-start | bytes 147464 | tf_op jit(solution)/shard_map/ppermute | solution.py:278
  11.0 5.2 %collective-permute-start.3 = (bf16[3,32,128]{2,1,0:T(8,128)(2,1)S(1)}, bf16[3,32,128]{2,1,0:T(8,128)(2,1)S(1)}, u32[]{:S(2)}, u32[]{:S(2)}) collective-permute-start(bf16[3,32,128]{2,1,0:T(8,128)(2,1)S(1)} %get-tuple-element.42.rest_0_.a_ref), channel_id=1, source_target_pairs={{0,64},{16,80},{32,96},{48,112},{64,0},{80,16},{96,32},{112,48},{1... | collective-permute-start | bytes 73736 | tf_op jit(solution)/shard_map/ppermute | solution.py:278
  13.2 7.8 %collective-permute-start.6 = (bf16[32,128]{1,0:T(8,128)(2,1)S(1)}, bf16[32,128]{1,0:T(8,128)(2,1)S(1)}, u32[]{:S(2)}, u32[]{:S(2)}) collective-permute-start(bf16[32,128]{1,0:T(8,128)(2,1)S(1)} %get-tuple-element.45.a_ref), channel_id=1, source_target_pairs={{0,4},{1,5},{2,6},{3,7},{4,0},{5,1},{6,2},{7,3},{8,12},{9,13},{10,... | collective-permute-start | bytes 24584 | tf_op jit(solution)/shard_map/ppermute | solution.py:278
  16.2 6.5 %collective-permute-start.5 = (bf16[3,64,128]{2,1,0:T(8,128)(2,1)S(1)}, bf16[3,64,128]{2,1,0:T(8,128)(2,1)S(1)}, u32[]{:S(2)}, u32[]{:S(2)}) collective-permute-start(bf16[3,64,128]{2,1,0:T(8,128)(2,1)S(1)} %shard_map.32._.rest_0_.a_ref), channel_id=1, source_target_pairs={{0,192},{16,208},{32,224},{48,240},{64,128},{80,144},{96,160},{112... | collective-permute-start | bytes 147464 | tf_op jit(solution)/shard_map/ppermute | solution.py:278
  19.7 7.2 %collective-permute-start.4 = (bf16[3,128,128]{2,1,0:T(8,128)(2,1)S(1)}, bf16[3,128,128]{2,1,0:T(8,128)(2,1)S(1)}, u32[]{:S(2)}, u32[]{:S(2)}) collective-permute-start(bf16[3,128,128]{2,1,0:T(8,128)(2,1)S(1)} %get-tuple-element.44.rest_0_.a_ref), channel_id=1, source_target_pairs={{0,64},{16,80},{32,96},{48,112},{64,0},{80,16},{96,32},{112,48},{1... | collective-permute-start | bytes 294920 | tf_op jit(solution)/shard_map/ppermute | solution.py:278
  22.7 6.8 %collective-permute-start.9 = (bf16[3,128,128]{2,1,0:T(8,128)(2,1)S(1)}, bf16[3,128,128]{2,1,0:T(8,128)(2,1)S(1)}, u32[]{:S(2)}, u32[]{:S(2)}) collective-permute-start(bf16[3,128,128]{2,1,0:T(8,128)(2,1)S(1)} %shard_map.36.rest_0_.token_ref.a_ref), channel_id=1, source_target_pairs={{0,1},{1,0},{2,3},{3,2},{4,5},{5,4},{6,7},{7,6},{8,9},{9,8},{10,11... | collective-permute-start | bytes 294920 | tf_op jit(solution)/shard_map/ppermute | solution.py:278
  24.0 18.8 %collective-permute-start.7 = (bf16[2,128,768]{2,1,0:T(8,128)(2,1)S(1)}, bf16[2,128,768]{2,1,0:T(8,128)(2,1)S(1)}, u32[]{:S(2)}, u32[]{:S(2)}) collective-permute-start(bf16[2,128,768]{2,1,0:T(8,128)(2,1)S(1)} %shard_map.38.rest_1_.own_ref), channel_id=1, source_target_pairs={{0,32},{16,48},{32,0},{48,16},{64,96},{80,112},{96,64},{112,80},{1... | collective-permute-start | bytes 1179656 | tf_op jit(solution)/shard_map/ppermute | solution.py:278
  28.6 0.9 %copy-start.2 = (f32[2,128,768]{2,1,0:T(8,128)}, f32[2,128,768]{2,1,0:T(8,128)S(1)}, u32[]{:S(2)}) copy-start(f32[2,128,768]{2,1,0:T(8,128)S(1)} %get-tuple-element.56.oe_ref) | copy-start | bytes 2359300
  29.5 9.5 %collective-permute-start.10 = (bf16[3,256,128]{2,1,0:T(8,128)(2,1)S(1)}, bf16[3,256,128]{2,1,0:T(8,128)(2,1)S(1)}, u32[]{:S(2)}, u32[]{:S(2)}) collective-permute-start(bf16[3,256,128]{2,1,0:T(8,128)(2,1)S(1)} %shard_map.40.token_ref.kv0_ref.four0_ref), channel_id=1, source_target_pairs={{0,2},{1,3},{2,0},{3,1},{4,6},{5,7},{6,4},{7,5},{8,10},{9,11},{10,... | collective-permute-start | bytes 589832 | tf_op jit(solution)/shard_map/ppermute | solution.py:278
  32.4 8.2 %collective-permute-start.8 = (bf16[3,256,128]{2,1,0:T(8,128)(2,1)S(1)}, bf16[3,256,128]{2,1,0:T(8,128)(2,1)S(1)}, u32[]{:S(2)}, u32[]{:S(2)}) collective-permute-start(bf16[3,256,128]{2,1,0:T(8,128)(2,1)S(1)} %shard_map.37.rest_0_.three0_ref), channel_id=1, source_target_pairs={{0,192},{16,208},{32,224},{48,240},{64,128},{80,144},{96,160},{112... | collective-permute-start | bytes 589832 | tf_op jit(solution)/shard_map/ppermute | solution.py:278
  32.4 6.6 %collective-permute-start.11 = (bf16[64,128]{1,0:T(8,128)(2,1)S(1)}, bf16[64,128]{1,0:T(8,128)(2,1)S(1)}, u32[]{:S(2)}, u32[]{:S(2)}) collective-permute-start(bf16[64,128]{1,0:T(8,128)(2,1)S(1)} %shard_map.41.q0_ref), channel_id=1, source_target_pairs={{0,8},{1,9},{2,10},{3,11},{4,12},{5,13},{6,14},{7,15},{8,0},{9,1},... | collective-permute-start | bytes 49160 | tf_op jit(solution)/shard_map/ppermute | solution.py:278
  34.6 18.3 %collective-permute-start.12 = (bf16[2,128,768]{2,1,0:T(8,128)(2,1)S(1)}, bf16[2,128,768]{2,1,0:T(8,128)(2,1)S(1)}, u32[]{:S(2)}, u32[]{:S(2)}) collective-permute-start(bf16[2,128,768]{2,1,0:T(8,128)(2,1)S(1)} %shard_map.38.rest_1_.own_ref), channel_id=1, source_target_pairs={{0,16},{16,0},{32,48},{48,32},{64,80},{80,64},{96,112},{112,96},{1... | collective-permute-start | bytes 1179656 | tf_op jit(solution)/shard_map/ppermute | solution.py:278
  42.9 10.1 %collective-permute-start.13 = (bf16[2,128,768]{2,1,0:T(8,128)(2,1)S(1)}, bf16[2,128,768]{2,1,0:T(8,128)(2,1)S(1)}, u32[]{:S(2)}, u32[]{:S(2)}) collective-permute-start(bf16[2,128,768]{2,1,0:T(8,128)(2,1)S(1)} %shard_map.44.r1_ref), channel_id=1, source_target_pairs={{0,16},{16,0},{32,48},{48,32},{64,80},{80,64},{96,112},{112,96},{1... | collective-permute-start | bytes 1179656 | tf_op jit(solution)/shard_map/ppermute | solution.py:278
  44.9 11.7 %all-to-all-start = ((f32[16,8,128]{2,1,0:T(8,128)}), f32[16,8,128]{2,1,0:T(8,128)S(1)}, u32[]{:S(2)}, u32[]{:S(2)}) async-start(f32[16,8,128]{2,1,0:T(8,128)} %shard_map.42._), calls=%async_computation | async-start | bytes 131072 | tf_op jit(solution)/shard_map/all_to_all | solution.py:344
  50.8 5.7 %collective-permute-start.14 = (f32[3,32,128]{2,1,0:T(8,128)}, f32[3,32,128]{2,1,0:T(8,128)S(1)}, u32[]{:S(2)}, u32[]{:S(2)}) collective-permute-start(f32[3,32,128]{2,1,0:T(8,128)} %get-tuple-element.62), channel_id=1, source_target_pairs={{0,16},{16,0},{32,48},{48,32},{64,80},{80,64},{96,112},{112,96},{1... | collective-permute-start | bytes 147464 | tf_op jit(solution)/shard_map/ppermute | solution.py:278
  51.0 5.5 %collective-permute-start.15 = (f32[3,32,128]{2,1,0:T(8,128)}, f32[3,32,128]{2,1,0:T(8,128)S(1)}, u32[]{:S(2)}, u32[]{:S(2)}) collective-permute-start(f32[3,32,128]{2,1,0:T(8,128)} %get-tuple-element.63), channel_id=1, source_target_pairs={{0,32},{16,48},{32,0},{48,16},{64,96},{80,112},{96,64},{112,80},{1... | collective-permute-start | bytes 147464 | tf_op jit(solution)/shard_map/ppermute | solution.py:278
  52.5 4.1 %collective-permute-start.16 = (f32[3,32,128]{2,1,0:T(8,128)}, f32[3,32,128]{2,1,0:T(8,128)S(1)}, u32[]{:S(2)}, u32[]{:S(2)}) collective-permute-start(f32[3,32,128]{2,1,0:T(8,128)} %get-tuple-element.64), channel_id=1, source_target_pairs={{0,48},{16,32},{32,16},{48,0},{64,112},{80,96},{96,80},{112,64},{1... | collective-permute-start | bytes 147464 | tf_op jit(solution)/shard_map/ppermute | solution.py:278
  52.9 1.1 %copy-start.3 = (f32[2,128,768]{2,1,0:T(8,128)S(1)}, f32[2,128,768]{2,1,0:T(8,128)}, u32[]{:S(2)}) copy-start(f32[2,128,768]{2,1,0:T(8,128)} %copy-done.2) | copy-start | bytes 2359300

commit v3 on v2

--- a/solution.py
+++ b/solution.py
@@ -74,18 +74,22 @@
 
 
 def sort_kernel(q_ref, kv_ref, qs_ref, ks_ref, vs_ref, send_ref):
-    row = lax.broadcasted_iota(jnp.int32, (ROWS, ROWS), 0)
+    row = lax.broadcasted_iota(jnp.int32, (ROWS, 1), 0)
     col = lax.broadcasted_iota(jnp.int32, (ROWS, ROWS), 1)
     onehot = (col == sorted_position(row)).astype(F32).astype(BF)
     half = lanes((128, 128)) < HEAD
-    for pair in range(HEADS // 2):
-        cols = pl.ds(pair * 128, 128)
-        a, b = (2 * pair) % 4 * 128, (2 * pair + 1) % 4 * 128
+    for third in range(3):
+        cols = pl.ds(third * 256, 256)
         qs_ref[:, cols] = dot(onehot, q_ref[0, :, cols]).astype(BF)
         for n, ref in ((0, ks_ref), (1, vs_ref)):
             x = dot(onehot, kv_ref[n, 0, :, cols])
             ref[:, cols] = x.astype(BF)
-            send_ref[n, :, cols] = jnp.where(half, x[a : a + 128], x[b : b + 128]).astype(BF)
+            for side in range(2):
+                part = slice(side * 128, side * 128 + 128)
+                a = side * 256
+                send_ref[n, :, pl.ds(third * 256 + side * 128, 128)] = jnp.where(
+                    half, x[a : a + 128, part], x[a + 128 : a + 256, part]
+                ).astype(BF)
 
 
 def attend_pair(q, k, v):
@@ -136,7 +140,7 @@
         o_ref[:, cols] = o[low : low + 32]
         e_ref[:, cols] = e[low : low + 32]
     row = lax.broadcasted_iota(jnp.int32, (ROWS, ROWS), 0)
-    col = lax.broadcasted_iota(jnp.int32, (ROWS, ROWS), 1)
+    col = lax.broadcasted_iota(jnp.int32, (1, ROWS), 1)
     unsort_ref[...] = (row == sorted_position(col)).astype(F32).astype(BF)
 
 

time: 58.7 us -> 58.7 us (level)
  Pallas kernels: 16.4 us -> 15.2 us
  waiting for transfers between devices: 2.41 us -> 3.6 us
    pallas_call x19, Pallas kernels: 16.4 us -> 15.2 us  [run(): pl.pallas_call(kernel, out_shape=[jax.ShapeDtypeStruct(s, d) for s, d in...]
    ppermute x17, waiting for transfers between devices: 2.4 us -> 3.59 us  [permute(): lax.ppermute(x, axis, [(i, partner(i)) for i in range(lax.axis_size(axis))])]
  transfers between devices with their start and end apart: 18 -> 18, of which waited for: 3 -> 3; matrix products, arithmetic and copies ran while one was open for 0% -> 0% of each run, Pallas kernels for 24% -> 22%
where the time goes in v3:
time: 58.7 us; the launch traced here: 58.4 us
  starting transfers between devices  34.9 us (59%)
  Pallas kernels  15.2 us (26%)
  local copies, waits for them, and re-layouts  4.55 us (8%)
  waiting for transfers between devices  3.6 us (6%)
    ppermute x17, starting transfers between devices, permute(): lax.ppermute(x, axis, [(i, partner(i)) for i in range(lax.axis_size(axis))])  29.2 us
    pallas_call x19, Pallas kernels, run(): pl.pallas_call(kernel, out_shape=[jax.ShapeDtypeStruct(s, d) for s, d in...  15.2 us
    all_to_all x1, starting transfers between devices, per_device(): spread = lax.all_to_all(fifth, ('gx', 'gy'), 0, 0, axis_index_groups=groups)  5.71 us
    unnamed x8, local copies, waits for them, and re-layouts  4.55 us
    ppermute x17, waiting for transfers between devices, permute(): lax.ppermute(x, axis, [(i, partner(i)) for i in range(lax.axis_size(axis))])  3.59 us
  transfers between devices with their start and end apart: 18, of which 3 were waited for; matrix products, arithmetic and copies ran while one was open for 0% of the time, Pallas kernels for 22%

profile of v3, /device:TPU:1, one launch (start us, length us, event | category | flops | bytes accessed | tf_op | source)
XLA Modules:
  0.0 58.4 jit_solution(10920075291366208246)
XLA Ops:
  0.0 1.4 %copy-done = bf16[2,1,512,768]{3,2,1,0:T(8,128)(2,1)S(1)} copy-done((bf16[2,1,512,768]{3,2,1,0:T(8,128)(2,1)S(1)}, bf16[2,1,512,768]{3,2,1,0:T(8,128)(2,1)}, u32[]{:S(2)}) %copy-start) | copy-done | bytes 1572888
  3.1 3.3 %collective-permute-start = (bf16[3,2,32,128]{3,2,1,0:T(8,128)(2,1)S(1)}, bf16[3,2,32,128]{3,2,1,0:T(8,128)(2,1)S(1)}, u32[]{:S(2)}, u32[]{:S(2)}) collective-permute-start(bf16[3,2,32,128]{3,2,1,0:T(8,128)(2,1)S(1)} %get-tuple-element.39), channel_id=1, source_target_pairs={{0,16},{16,0},{32,48},{48,32},{64,80},{80,64},{96,112},{112,96},{1... | collective-permute-start | bytes 147464 | tf_op jit(solution)/shard_map/ppermute | solution.py:282
  6.4 1.7 %collective-permute-start.2 = (bf16[3,2,32,128]{3,2,1,0:T(8,128)(2,1)S(1)}, bf16[3,2,32,128]{3,2,1,0:T(8,128)(2,1)S(1)}, u32[]{:S(2)}, u32[]{:S(2)}) collective-permute-start(bf16[3,2,32,128]{3,2,1,0:T(8,128)(2,1)S(1)} %get-tuple-element.41), channel_id=1, source_target_pairs={{0,48},{16,32},{32,16},{48,0},{64,112},{80,96},{96,80},{112,64},{1... | collective-permute-start | bytes 147464 | tf_op jit(solution)/shard_map/ppermute | solution.py:282
  8.2 1.5 %shard_map.28 = (bf16[512,768]{1,0:T(8,128)(2,1)S(1)}, bf16[512,768]{1,0:T(8,128)(2,1)S(1)}, bf16[512,768]{1,0:T(8,128)(2,1)S(1)}, bf16[2,128,768]{2,1,0:T(8,128)(2,1)S(1)}) custom-call(bf16[1,512,768]{2,1,0:T(8,128)(2,1)S(1)} %copy-done.1, bf16[2,1,512,768]{3,2,1,0:T(8,128)(2,1)S(1)} %copy-done), custom_call_target="tpu_custom_call" | custom-call | bytes 6291456 | tf_op jit(solution)/shard_map/pallas_call | solution.py:267
  9.7 1.3 %collective-permute-done.2.r3_ref = bf16[3,2,32,128]{3,2,1,0:T(8,128)(2,1)S(1)} collective-permute-done((bf16[3,2,32,128]{3,2,1,0:T(8,128)(2,1)S(1)}, bf16[3,2,32,128]{3,2,1,0:T(8,128)(2,1)S(1)}, u32[]{:S(2)}, u32[]{:S(2)}) %collective-permute-start.2) | collective-permute-done | bytes 49184 | tf_op jit(solution)/shard_map/ppermute | solution.py:282
  11.0 2.2 %collective-permute-start.3 = (bf16[3,32,128]{2,1,0:T(8,128)(2,1)S(1)}, bf16[3,32,128]{2,1,0:T(8,128)(2,1)S(1)}, u32[]{:S(2)}, u32[]{:S(2)}) collective-permute-start(bf16[3,32,128]{2,1,0:T(8,128)(2,1)S(1)} %get-tuple-element.42.rest_0_.a_ref), channel_id=1, source_target_pairs={{0,64},{16,80},{32,96},{48,112},{64,0},{80,16},{96,32},{112,48},{1... | collective-permute-start | bytes 73736 | tf_op jit(solution)/shard_map/ppermute | solution.py:282
  13.2 1.3 %collective-permute-start.6 = (bf16[32,128]{1,0:T(8,128)(2,1)S(1)}, bf16[32,128]{1,0:T(8,128)(2,1)S(1)}, u32[]{:S(2)}, u32[]{:S(2)}) collective-permute-start(bf16[32,128]{1,0:T(8,128)(2,1)S(1)} %get-tuple-element.45.a_ref), channel_id=1, source_target_pairs={{0,4},{1,5},{2,6},{3,7},{4,0},{5,1},{6,2},{7,3},{8,12},{9,13},{10,... | collective-permute-start | bytes 24584 | tf_op jit(solution)/shard_map/ppermute | solution.py:282
  14.5 1.7 %shard_map.31 = (bf16[512,768]{1,0:T(8,128)(2,1)S(1)}, f32[2,128,768]{2,1,0:T(8,128)S(1)}, bf16[128,768]{1,0:T(8,128)(2,1)S(1)}) custom-call(bf16[512,768]{1,0:T(8,128)(2,1)S(1)} %get-tuple-element.35.q_ref, bf16[512,768]{1,0:T(8,128)(2,1)S(1)} %get-tuple-element.36.k_ref, bf16[512,768]{1,0:T(8,128)(2,1)S(1)} %get-tuple-element.37.v_ref, ...), custom_call_target="tpu_custom_call" | custom-call | flops 2147483648 | bytes 262144 | tf_op jit(solution)/shard_map/pallas_call | solution.py:267
  16.2 3.5 %collective-permute-start.5 = (bf16[3,64,128]{2,1,0:T(8,128)(2,1)S(1)}, bf16[3,64,128]{2,1,0:T(8,128)(2,1)S(1)}, u32[]{:S(2)}, u32[]{:S(2)}) collective-permute-start(bf16[3,64,128]{2,1,0:T(8,128)(2,1)S(1)} %shard_map.32._.rest_0_.a_ref), channel_id=1, source_target_pairs={{0,192},{16,208},{32,224},{48,240},{64,128},{80,144},{96,160},{112... | collective-permute-start | bytes 147464 | tf_op jit(solution)/shard_map/ppermute | solution.py:282
  19.7 1.3 %collective-permute-start.4 = (bf16[3,128,128]{2,1,0:T(8,128)(2,1)S(1)}, bf16[3,128,128]{2,1,0:T(8,128)(2,1)S(1)}, u32[]{:S(2)}, u32[]{:S(2)}) collective-permute-start(bf16[3,128,128]{2,1,0:T(8,128)(2,1)S(1)} %get-tuple-element.44.rest_0_.a_ref), channel_id=1, source_target_pairs={{0,64},{16,80},{32,96},{48,112},{64,0},{80,16},{96,32},{112,48},{1... | collective-permute-start | bytes 294920 | tf_op jit(solution)/shard_map/ppermute | solution.py:282
  21.0 1.7 %shard_map.35 = (bf16[512,768]{1,0:T(8,128)(2,1)S(1)}, f32[2,128,768]{2,1,0:T(8,128)S(1)}, bf16[128,768]{1,0:T(8,128)(2,1)S(1)}) custom-call(bf16[512,768]{1,0:T(8,128)(2,1)S(1)} %get-tuple-element.35.q_ref, bf16[512,768]{1,0:T(8,128)(2,1)S(1)} %get-tuple-element.36.k_ref, ...), custom_call_target="tpu_custom_call", output_to_operand_aliasing={{0}: (5, {}), {1}: (6, {}), {2}: (7, {})} | custom-call | flops 2147483648 | bytes 262144 | tf_op jit(solution)/shard_map/pallas_call | solution.py:267
  22.7 1.3 %collective-permute-start.9 = (bf16[3,128,128]{2,1,0:T(8,128)(2,1)S(1)}, bf16[3,128,128]{2,1,0:T(8,128)(2,1)S(1)}, u32[]{:S(2)}, u32[]{:S(2)}) collective-permute-start(bf16[3,128,128]{2,1,0:T(8,128)(2,1)S(1)} %shard_map.36.rest_0_.token_ref.a_ref), channel_id=1, source_target_pairs={{0,1},{1,0},{2,3},{3,2},{4,5},{5,4},{6,7},{7,6},{8,9},{9,8},{10,11... | collective-permute-start | bytes 294920 | tf_op jit(solution)/shard_map/ppermute | solution.py:282
  24.7 2.2 %collective-permute-done.4.b_ref = bf16[3,128,128]{2,1,0:T(8,128)(2,1)S(1)} collective-permute-done((bf16[3,128,128]{2,1,0:T(8,128)(2,1)S(1)}, bf16[3,128,128]{2,1,0:T(8,128)(2,1)S(1)}, u32[]{:S(2)}, u32[]{:S(2)}) %collective-permute-start.4) | collective-permute-done | bytes 98336 | tf_op jit(solution)/shard_map/ppermute | solution.py:282
  26.9 1.7 %shard_map.39 = (bf16[512,768]{1,0:T(8,128)(2,1)S(1)}, f32[2,128,768]{2,1,0:T(8,128)S(1)}, bf16[128,768]{1,0:T(8,128)(2,1)S(1)}) custom-call(bf16[512,768]{1,0:T(8,128)(2,1)S(1)} %get-tuple-element.35.q_ref, bf16[512,768]{1,0:T(8,128)(2,1)S(1)} %get-tuple-element.36.k_ref, ...), custom_call_target="tpu_custom_call", output_to_operand_aliasing={{0}: (5, {}), {1}: (6, {}), {2}: (7, {})} | custom-call | flops 2147483648 | bytes 262144 | tf_op jit(solution)/shard_map/pallas_call | solution.py:267
  29.5 3.0 %collective-permute-start.10 = (bf16[3,256,128]{2,1,0:T(8,128)(2,1)S(1)}, bf16[3,256,128]{2,1,0:T(8,128)(2,1)S(1)}, u32[]{:S(2)}, u32[]{:S(2)}) collective-permute-start(bf16[3,256,128]{2,1,0:T(8,128)(2,1)S(1)} %shard_map.40.token_ref.kv0_ref.four0_ref), channel_id=1, source_target_pairs={{0,2},{1,3},{2,0},{3,1},{4,6},{5,7},{6,4},{7,5},{8,10},{9,11},{10,... | collective-permute-start | bytes 589832 | tf_op jit(solution)/shard_map/ppermute | solution.py:282
  32.5 2.3 %collective-permute-start.11 = (bf16[64,128]{1,0:T(8,128)(2,1)S(1)}, bf16[64,128]{1,0:T(8,128)(2,1)S(1)}, u32[]{:S(2)}, u32[]{:S(2)}) collective-permute-start(bf16[64,128]{1,0:T(8,128)(2,1)S(1)} %shard_map.41.q0_ref), channel_id=1, source_target_pairs={{0,8},{1,9},{2,10},{3,11},{4,12},{5,13},{6,14},{7,15},{8,0},{9,1},... | collective-permute-start | bytes 49160 | tf_op jit(solution)/shard_map/ppermute | solution.py:282
  34.8 4.3 %collective-permute-start.12 = (bf16[2,128,768]{2,1,0:T(8,128)(2,1)S(1)}, bf16[2,128,768]{2,1,0:T(8,128)(2,1)S(1)}, u32[]{:S(2)}, u32[]{:S(2)}) collective-permute-start(bf16[2,128,768]{2,1,0:T(8,128)(2,1)S(1)} %shard_map.38.rest_1_.own_ref), channel_id=1, source_target_pairs={{0,16},{16,0},{32,48},{48,32},{64,80},{80,64},{96,112},{112,96},{1... | collective-permute-start | bytes 1179656 | tf_op jit(solution)/shard_map/ppermute | solution.py:282
  39.1 1.6 %shard_map.42._ = f32[16,8,128]{2,1,0:T(8,128)} custom-call(bf16[64,128]{1,0:T(8,128)(2,1)S(1)} %shard_map.41.q0_ref, bf16[64,128]{1,0:T(8,128)(2,1)S(1)} %collective-permute-done.11.q1_ref, bf16[3,256,128]{2,1,0:T(8,128)(2,1)S(1)} %shard_map.40.token_ref.kv0_ref.four0_ref, bf16[3,256,128]{2,1,0:T(8,128)(2,1)S(1)} %collective-permute-done.10.kv1_ref.four1_ref), custom_call_target="tpu_custom_call" | custom-call | bytes 1048576 | tf_op jit(solution)/shard_map/pallas_call | solution.py:267
  40.7 2.3 %shard_map.43 = (f32[3,32,128]{2,1,0:T(8,128)S(1)}, f32[3,32,128]{2,1,0:T(8,128)}, f32[3,32,128]{2,1,0:T(8,128)}, f32[3,32,128]{2,1,0:T(8,128)}) custom-call(bf16[3,128,128]{2,1,0:T(8,128)(2,1)S(1)} %get-tuple-element.53.q_ref, bf16[3,256,128]{2,1,0:T(8,128)(2,1)S(1)} %shard_map.37.rest_0_.three0_ref, ...), custom_call_target="tpu_custom_call" | custom-call | bytes 1048576 | tf_op jit(solution)/shard_map/pallas_call | solution.py:267
  43.0 2.0 %collective-permute-start.13 = (bf16[2,128,768]{2,1,0:T(8,128)(2,1)S(1)}, bf16[2,128,768]{2,1,0:T(8,128)(2,1)S(1)}, u32[]{:S(2)}, u32[]{:S(2)}) collective-permute-start(bf16[2,128,768]{2,1,0:T(8,128)(2,1)S(1)} %shard_map.44.r1_ref), channel_id=1, source_target_pairs={{0,16},{16,0},{32,48},{48,32},{64,80},{80,64},{96,112},{112,96},{1... | collective-permute-start | bytes 1179656 | tf_op jit(solution)/shard_map/ppermute | solution.py:282
  45.1 5.7 %all-to-all-start = ((f32[16,8,128]{2,1,0:T(8,128)}), f32[16,8,128]{2,1,0:T(8,128)S(1)}, u32[]{:S(2)}, u32[]{:S(2)}) async-start(f32[16,8,128]{2,1,0:T(8,128)} %shard_map.42._), calls=%async_computation | async-start | bytes 131072 | tf_op jit(solution)/shard_map/all_to_all | solution.py:348
  51.0 1.6 %collective-permute-start.15 = (f32[3,32,128]{2,1,0:T(8,128)}, f32[3,32,128]{2,1,0:T(8,128)S(1)}, u32[]{:S(2)}, u32[]{:S(2)}) collective-permute-start(f32[3,32,128]{2,1,0:T(8,128)} %get-tuple-element.63), channel_id=1, source_target_pairs={{0,32},{16,48},{32,0},{48,16},{64,96},{80,112},{96,64},{112,80},{1... | collective-permute-start | bytes 147464 | tf_op jit(solution)/shard_map/ppermute | solution.py:282
  54.1 2.4 %shard_map.45 = (bf16[512,768]{1,0:T(8,128)(2,1)S(1)}, f32[32,768]{1,0:T(8,128)S(1)}, f32[32,768]{1,0:T(8,128)S(1)}, bf16[512,512]{1,0:T(8,128)(2,1)S(1)}) custom-call(bf16[128,768]{1,0:T(8,128)(2,1)S(1)} %get-tuple-element.52.rest_0_.q_ref, bf16[2,128,768]{2,1,0:T(8,128)(2,1)S(1)} %shard_map.38.rest_1_.own_ref, ...), custom_call_target="tpu_custom_call", output_to_operand_aliasing={{0}: (6, {})} | custom-call | flops 2147483648 | bytes 3145728 | tf_op jit(solution)/shard_map/pallas_call | solution.py:267
  56.6 1.8 %shard_map.46 = bf16[1,512,768]{2,1,0:T(8,128)(2,1)} custom-call(bf16[512,768]{1,0:T(8,128)(2,1)S(1)} %get-tuple-element.58.a_ref, f32[32,768]{1,0:T(8,128)S(1)} %get-tuple-element.59.o_ref, f32[32,768]{1,0:T(8,128)S(1)} %get-tuple-element.60.e_ref, bf16[512,512]{1,0:T(8,128)(2,1)S(1)} %get-tuple-element.61.unsort_ref, ...), custom_call_target="tpu_custom_call" | custom-call | bytes 4194304 | tf_op jit(solution)/shard_map/pallas_call | solution.py:267
  (39 shorter events, 5.2 us)
Async XLA Ops:
  0.0 1.4 %copy-start = (bf16[2,1,512,768]{3,2,1,0:T(8,128)(2,1)S(1)}, bf16[2,1,512,768]{3,2,1,0:T(8,128)(2,1)}, u32[]{:S(2)}) copy-start(bf16[2,1,512,768]{3,2,1,0:T(8,128)(2,1)} %kv_ref.3) | copy-start | bytes 4718596
  1.4 1.1 %copy-start.1 = (bf16[1,512,768]{2,1,0:T(8,128)(2,1)S(1)}, bf16[1,512,768]{2,1,0:T(8,128)(2,1)}, u32[]{:S(2)}) copy-start(bf16[1,512,768]{2,1,0:T(8,128)(2,1)} %q_ref.3) | copy-start | bytes 2359300
  3.1 6.6 %collective-permute-start = (bf16[3,2,32,128]{3,2,1,0:T(8,128)(2,1)S(1)}, bf16[3,2,32,128]{3,2,1,0:T(8,128)(2,1)S(1)}, u32[]{:S(2)}, u32[]{:S(2)}) collective-permute-start(bf16[3,2,32,128]{3,2,1,0:T(8,128)(2,1)S(1)} %get-tuple-element.39), channel_id=1, source_target_pairs={{0,16},{16,0},{32,48},{48,32},{64,80},{80,64},{96,112},{112,96},{1... | collective-permute-start | bytes 147464 | tf_op jit(solution)/shard_map/ppermute | solution.py:282
  6.4 3.2 %collective-permute-start.1 = (bf16[3,2,32,128]{3,2,1,0:T(8,128)(2,1)S(1)}, bf16[3,2,32,128]{3,2,1,0:T(8,128)(2,1)S(1)}, u32[]{:S(2)}, u32[]{:S(2)}) collective-permute-start(bf16[3,2,32,128]{3,2,1,0:T(8,128)(2,1)S(1)} %get-tuple-element.40), channel_id=1, source_target_pairs={{0,32},{16,48},{32,0},{48,16},{64,96},{80,112},{96,64},{112,80},{1... | collective-permute-start | bytes 147464 | tf_op jit(solution)/shard_map/ppermute | solution.py:282
  6.4 4.5 %collective-permute-start.2 = (bf16[3,2,32,128]{3,2,1,0:T(8,128)(2,1)S(1)}, bf16[3,2,32,128]{3,2,1,0:T(8,128)(2,1)S(1)}, u32[]{:S(2)}, u32[]{:S(2)}) collective-permute-start(bf16[3,2,32,128]{3,2,1,0:T(8,128)(2,1)S(1)} %get-tuple-element.41), channel_id=1, source_target_pairs={{0,48},{16,32},{32,16},{48,0},{64,112},{80,96},{96,80},{112,64},{1... | collective-permute-start | bytes 147464 | tf_op jit(solution)/shard_map/ppermute | solution.py:282
  11.0 5.2 %collective-permute-start.3 = (bf16[3,32,128]{2,1,0:T(8,128)(2,1)S(1)}, bf16[3,32,128]{2,1,0:T(8,128)(2,1)S(1)}, u32[]{:S(2)}, u32[]{:S(2)}) collective-permute-start(bf16[3,32,128]{2,1,0:T(8,128)(2,1)S(1)} %get-tuple-element.42.rest_0_.a_ref), channel_id=1, source_target_pairs={{0,64},{16,80},{32,96},{48,112},{64,0},{80,16},{96,32},{112,48},{1... | collective-permute-start | bytes 73736 | tf_op jit(solution)/shard_map/ppermute | solution.py:282
  13.2 7.8 %collective-permute-start.6 = (bf16[32,128]{1,0:T(8,128)(2,1)S(1)}, bf16[32,128]{1,0:T(8,128)(2,1)S(1)}, u32[]{:S(2)}, u32[]{:S(2)}) collective-permute-start(bf16[32,128]{1,0:T(8,128)(2,1)S(1)} %get-tuple-element.45.a_ref), channel_id=1, source_target_pairs={{0,4},{1,5},{2,6},{3,7},{4,0},{5,1},{6,2},{7,3},{8,12},{9,13},{10,... | collective-permute-start | bytes 24584 | tf_op jit(solution)/shard_map/ppermute | solution.py:282
  16.2 6.5 %collective-permute-start.5 = (bf16[3,64,128]{2,1,0:T(8,128)(2,1)S(1)}, bf16[3,64,128]{2,1,0:T(8,128)(2,1)S(1)}, u32[]{:S(2)}, u32[]{:S(2)}) collective-permute-start(bf16[3,64,128]{2,1,0:T(8,128)(2,1)S(1)} %shard_map.32._.rest_0_.a_ref), channel_id=1, source_target_pairs={{0,192},{16,208},{32,224},{48,240},{64,128},{80,144},{96,160},{112... | collective-permute-start | bytes 147464 | tf_op jit(solution)/shard_map/ppermute | solution.py:282
  19.7 7.2 %collective-permute-start.4 = (bf16[3,128,128]{2,1,0:T(8,128)(2,1)S(1)}, bf16[3,128,128]{2,1,0:T(8,128)(2,1)S(1)}, u32[]{:S(2)}, u32[]{:S(2)}) collective-permute-start(bf16[3,128,128]{2,1,0:T(8,128)(2,1)S(1)} %get-tuple-element.44.rest_0_.a_ref), channel_id=1, source_target_pairs={{0,64},{16,80},{32,96},{48,112},{64,0},{80,16},{96,32},{112,48},{1... | collective-permute-start | bytes 294920 | tf_op jit(solution)/shard_map/ppermute | solution.py:282
  22.7 6.8 %collective-permute-start.9 = (bf16[3,128,128]{2,1,0:T(8,128)(2,1)S(1)}, bf16[3,128,128]{2,1,0:T(8,128)(2,1)S(1)}, u32[]{:S(2)}, u32[]{:S(2)}) collective-permute-start(bf16[3,128,128]{2,1,0:T(8,128)(2,1)S(1)} %shard_map.36.rest_0_.token_ref.a_ref), channel_id=1, source_target_pairs={{0,1},{1,0},{2,3},{3,2},{4,5},{5,4},{6,7},{7,6},{8,9},{9,8},{10,11... | collective-permute-start | bytes 294920 | tf_op jit(solution)/shard_map/ppermute | solution.py:282
  24.0 19.0 %collective-permute-start.7 = (bf16[2,128,768]{2,1,0:T(8,128)(2,1)S(1)}, bf16[2,128,768]{2,1,0:T(8,128)(2,1)S(1)}, u32[]{:S(2)}, u32[]{:S(2)}) collective-permute-start(bf16[2,128,768]{2,1,0:T(8,128)(2,1)S(1)} %shard_map.38.rest_1_.own_ref), channel_id=1, source_target_pairs={{0,32},{16,48},{32,0},{48,16},{64,96},{80,112},{96,64},{112,80},{1... | collective-permute-start | bytes 1179656 | tf_op jit(solution)/shard_map/ppermute | solution.py:282
  28.6 0.9 %copy-start.2 = (f32[2,128,768]{2,1,0:T(8,128)}, f32[2,128,768]{2,1,0:T(8,128)S(1)}, u32[]{:S(2)}) copy-start(f32[2,128,768]{2,1,0:T(8,128)S(1)} %get-tuple-element.56.oe_ref) | copy-start | bytes 2359300
  29.5 9.6 %collective-permute-start.10 = (bf16[3,256,128]{2,1,0:T(8,128)(2,1)S(1)}, bf16[3,256,128]{2,1,0:T(8,128)(2,1)S(1)}, u32[]{:S(2)}, u32[]{:S(2)}) collective-permute-start(bf16[3,256,128]{2,1,0:T(8,128)(2,1)S(1)} %shard_map.40.token_ref.kv0_ref.four0_ref), channel_id=1, source_target_pairs={{0,2},{1,3},{2,0},{3,1},{4,6},{5,7},{6,4},{7,5},{8,10},{9,11},{10,... | collective-permute-start | bytes 589832 | tf_op jit(solution)/shard_map/ppermute | solution.py:282
  32.5 8.2 %collective-permute-start.8 = (bf16[3,256,128]{2,1,0:T(8,128)(2,1)S(1)}, bf16[3,256,128]{2,1,0:T(8,128)(2,1)S(1)}, u32[]{:S(2)}, u32[]{:S(2)}) collective-permute-start(bf16[3,256,128]{2,1,0:T(8,128)(2,1)S(1)} %shard_map.37.rest_0_.three0_ref), channel_id=1, source_target_pairs={{0,192},{16,208},{32,224},{48,240},{64,128},{80,144},{96,160},{112... | collective-permute-start | bytes 589832 | tf_op jit(solution)/shard_map/ppermute | solution.py:282
  32.5 6.6 %collective-permute-start.11 = (bf16[64,128]{1,0:T(8,128)(2,1)S(1)}, bf16[64,128]{1,0:T(8,128)(2,1)S(1)}, u32[]{:S(2)}, u32[]{:S(2)}) collective-permute-start(bf16[64,128]{1,0:T(8,128)(2,1)S(1)} %shard_map.41.q0_ref), channel_id=1, source_target_pairs={{0,8},{1,9},{2,10},{3,11},{4,12},{5,13},{6,14},{7,15},{8,0},{9,1},... | collective-permute-start | bytes 49160 | tf_op jit(solution)/shard_map/ppermute | solution.py:282
  34.8 18.1 %collective-permute-start.12 = (bf16[2,128,768]{2,1,0:T(8,128)(2,1)S(1)}, bf16[2,128,768]{2,1,0:T(8,128)(2,1)S(1)}, u32[]{:S(2)}, u32[]{:S(2)}) collective-permute-start(bf16[2,128,768]{2,1,0:T(8,128)(2,1)S(1)} %shard_map.38.rest_1_.own_ref), channel_id=1, source_target_pairs={{0,16},{16,0},{32,48},{48,32},{64,80},{80,64},{96,112},{112,96},{1... | collective-permute-start | bytes 1179656 | tf_op jit(solution)/shard_map/ppermute | solution.py:282
  43.0 9.9 %collective-permute-start.13 = (bf16[2,128,768]{2,1,0:T(8,128)(2,1)S(1)}, bf16[2,128,768]{2,1,0:T(8,128)(2,1)S(1)}, u32[]{:S(2)}, u32[]{:S(2)}) collective-permute-start(bf16[2,128,768]{2,1,0:T(8,128)(2,1)S(1)} %shard_map.44.r1_ref), channel_id=1, source_target_pairs={{0,16},{16,0},{32,48},{48,32},{64,80},{80,64},{96,112},{112,96},{1... | collective-permute-start | bytes 1179656 | tf_op jit(solution)/shard_map/ppermute | solution.py:282
  45.1 11.5 %all-to-all-start = ((f32[16,8,128]{2,1,0:T(8,128)}), f32[16,8,128]{2,1,0:T(8,128)S(1)}, u32[]{:S(2)}, u32[]{:S(2)}) async-start(f32[16,8,128]{2,1,0:T(8,128)} %shard_map.42._), calls=%async_computation | async-start | bytes 131072 | tf_op jit(solution)/shard_map/all_to_all | solution.py:348
  50.8 5.7 %collective-permute-start.14 = (f32[3,32,128]{2,1,0:T(8,128)}, f32[3,32,128]{2,1,0:T(8,128)S(1)}, u32[]{:S(2)}, u32[]{:S(2)}) collective-permute-start(f32[3,32,128]{2,1,0:T(8,128)} %get-tuple-element.62), channel_id=1, source_target_pairs={{0,16},{16,0},{32,48},{48,32},{64,80},{80,64},{96,112},{112,96},{1... | collective-permute-start | bytes 147464 | tf_op jit(solution)/shard_map/ppermute | solution.py:282
  51.0 5.5 %collective-permute-start.15 = (f32[3,32,128]{2,1,0:T(8,128)}, f32[3,32,128]{2,1,0:T(8,128)S(1)}, u32[]{:S(2)}, u32[]{:S(2)}) collective-permute-start(f32[3,32,128]{2,1,0:T(8,128)} %get-tuple-element.63), channel_id=1, source_target_pairs={{0,32},{16,48},{32,0},{48,16},{64,96},{80,112},{96,64},{112,80},{1... | collective-permute-start | bytes 147464 | tf_op jit(solution)/shard_map/ppermute | solution.py:282
  52.5 4.1 %collective-permute-start.16 = (f32[3,32,128]{2,1,0:T(8,128)}, f32[3,32,128]{2,1,0:T(8,128)S(1)}, u32[]{:S(2)}, u32[]{:S(2)}) collective-permute-start(f32[3,32,128]{2,1,0:T(8,128)} %get-tuple-element.64), channel_id=1, source_target_pairs={{0,48},{16,32},{32,16},{48,0},{64,112},{80,96},{96,80},{112,64},{1... | collective-permute-start | bytes 147464 | tf_op jit(solution)/shard_map/ppermute | solution.py:282
  52.9 1.1 %copy-start.3 = (f32[2,128,768]{2,1,0:T(8,128)S(1)}, f32[2,128,768]{2,1,0:T(8,128)}, u32[]{:S(2)}) copy-start(f32[2,128,768]{2,1,0:T(8,128)} %copy-done.2) | copy-start | bytes 2359300
